TPU v7x, 32 devices: a whole 2x2x4 slice. The times are simulated.
32 devices in a mesh: dp: 8 (over z, core), tensor: 4 (over y, x).
Axes of the slice: x: 2, y: 2, z: 4, core: 2. Of those that a mesh axis runs over, the one named last changes fastest.
Arguments:
- activations: bfloat16 [8192, 8192], P('dp'), may hold values from -6 to 6
- out_grad: bfloat16 [8192, 28672], P('dp', 'tensor'), may hold values from -0.06591797 to 0.06591797
- projector: bfloat16 [8192, 512], P(('dp', 'tensor')), may hold values from -0.0625 to 0.0625
- first_moment: float32 [512, 28672], P('dp', 'tensor'), may hold values from -3 to 3
- second_moment: float32 [512, 28672], P('dp', 'tensor'), may hold values from 0.1 to 4
Outputs:
- update: float32 [8192, 28672], P('dp', 'tensor')
- new_first: float32 [512, 28672], P('dp', 'tensor')
- new_second: float32 [512, 28672], P('dp', 'tensor')
All inputs are finite; a program needn't handle non-finite values.
Results may differ from a plain program's by a relative error of at most 0.0031.
Values may be sent and summed in bfloat16 or wider, within the bound.
No kernel may reach another device: no remote copies, remote signals or barrier semaphores. Data moves between devices by JAX's collectives and lax.ppermute only.
A program may use at most 192 MiB of HBM per device.

v0:
```python
import jax
import jax.numpy as jnp
from jax import lax
from jax.sharding import PartitionSpec as P

beta_one = 0.9
beta_two = 0.999
bias_one = 1.0 - 0.9**10
bias_two = 1.0 - 0.999**10
adam_eps = 1e-08


def per_device(activations, out_grad, projector, first_moment, second_moment):
    columns = activations
    projected = jnp.dot(
        columns,
        lax.all_gather(projector, ("dp", "tensor"), axis=0, tiled=True),
        preferred_element_type=jnp.float32,
    )
    projected = projected.astype(jnp.bfloat16)
    coefficients = lax.psum_scatter(
        lax.dot_general(
            projected, out_grad, (((0,), (0,)), ((), ())), preferred_element_type=jnp.float32
        ),
        "dp",
        scatter_dimension=0,
        tiled=True,
    )
    new_first = beta_one * first_moment + (1.0 - beta_one) * coefficients
    new_second = beta_two * second_moment + (1.0 - beta_two) * coefficients * coefficients
    normalized = (new_first / bias_one / (jnp.sqrt(new_second / bias_two) + adam_eps)).astype(
        jnp.bfloat16
    )
    basis_rows = lax.all_gather(projector, "tensor", axis=0, tiled=True)
    columns = basis_rows
    update = jnp.dot(
        columns,
        lax.all_gather(normalized, "dp", axis=0, tiled=True),
        preferred_element_type=jnp.float32,
    )
    return (update, new_first, new_second)


def solution(mesh):
    in_specs = (
        P("dp", None),
        P("dp", "tensor"),
        P(("dp", "tensor"), None),
        P("dp", "tensor"),
        P("dp", "tensor"),
    )
    out_specs = (P("dp", "tensor"), P("dp", "tensor"), P("dp", "tensor"))
    return jax.shard_map(
        per_device, mesh=mesh, in_specs=in_specs, out_specs=out_specs, check_vma=False
    )
```

profile of v0, /device:TPU:16, one launch (start us, length us, event | category | flops | bytes accessed | tf_op | source)
XLA Modules:
  0.0 396.5 jit_solution(9395981226364708526)
XLA Ops:
  8.0 0.0 all-gather.4.cloned.1.call-start
  8.0 0.7 all-gather.4.cloned.1.call-update
  8.7 0.0 reduce-scatter.2.cloned.1.call-start
  8.8 81.1 %all-gather.4.cloned.1.call-done = bf16[8192,512]{1,0:T(8,128)(2,1)} async-done(((bf16[256,512]{1,0:T(8,128)(2,1)}), bf16[8192,512]{1,0:T(8,128)(2,1)}) %all-gather.4.cloned.1.call-update) | async-done | bytes 8388624 | tf_op jit(solution)/shard_map/all_gather | solution.py:17
  89.9 30.3 %fusion.1 = f32[512,7168]{1,0:T(8,128)} fusion(bf16[1024,7168]{1,0:T(8,128)(2,1)} %param.6, bf16[1024,8192]{1,0:T(8,128)(2,1)} %param.5, bf16[8192,512]{1,0:T(8,128)(2,1)} %all-gather.4.cloned.1.call-done), kind=kOutput, calls=%fused_computation.6 | convolution fusion | flops 16106651648 | bytes 54525952 | tf_op jit(solution)/shard_map/dot_general | solution.py:22
  120.1 0.0 copy-start
  120.1 0.0 reduce-scatter.2.cloned.1.call-update
  120.2 0.0 all-gather.8.cloned.1.call-start
  120.2 0.5 all-gather.8.cloned.1.call-update
  120.7 0.2 all-gather.6.cloned.1.call-start
  121.0 144.9 %reduce-scatter.2.cloned.1.call-done = f32[64,7168]{1,0:T(8,128)} async-done(((f32[512,7168]{1,0:T(8,128)}), f32[64,7168]{1,0:T(8,128)}) %reduce-scatter.2.cloned.1.call-update) | async-done | bytes 1835024 | tf_op jit(solution)/shard_map/reduce_scatter | solution.py:21
  265.9 0.0 copy-done
  265.9 4.8 %divide_convert_fusion = (bf16[64,7168]{1,0:T(8,128)(2,1)}, f32[64,7168]{1,0:T(8,128)}, f32[64,7168]{1,0:T(8,128)}) fusion(f32[64,7168]{1,0:T(8,128)} %reduce-scatter.2.cloned.1.call-done, f32[64,7168]{1,0:T(8,128)S(1)} %copy-done, f32[64,7168]{1,0:T(8,128)} %param.9), kind=kLoop, calls=%fused_computation.3 | loop fusion | flops 5505024 | bytes 10092544 | tf_op jit(solution)/shard_map/convert_element_type | solution.py:31
  270.7 0.0 all-gather.6.cloned.1.call-update
  270.7 0.0 all-gather.8.cloned.1.call-done
  270.8 72.8 %all-gather.6.cloned.1.call-done = bf16[512,7168]{1,0:T(8,128)(2,1)} async-done(((bf16[64,7168]{1,0:T(8,128)(2,1)}), bf16[512,7168]{1,0:T(8,128)(2,1)}) %all-gather.6.cloned.1.call-update) | async-done | bytes 7340048 | tf_op jit(solution)/shard_map/all_gather | solution.py:38
  343.6 15.9 %convolution_bitcast_fusion = f32[1024,7168]{0,1:T(8,128)} fusion(bf16[512,7168]{1,0:T(8,128)(2,1)} %all-gather.6.cloned.1.call-done, bf16[1024,512]{1,0:T(8,128)(2,1)} %all-gather.8.cloned.1.call-done), kind=kOutput, calls=%fused_computation | convolution fusion | flops 7516192768 | bytes 37748736 | tf_op jit(solution)/shard_map/dot_general | solution.py:36
  359.5 29.5 %copy.8 = f32[1024,7168]{1,0:T(8,128)} copy(f32[1024,7168]{0,1:T(8,128)} %convolution_bitcast_fusion) | data formatting | bytes 58720256
Async XLA Ops:
  8.0 81.9 %all-gather.4.cloned.1.call-start = ((), (), s32[]{:S(2)}) async-start(), calls=%async_computation.1 | async-start | bytes 8650752 | tf_op jit(solution)/shard_map/all_gather | solution.py:17
  8.7 257.1 %reduce-scatter.2.cloned.1.call-start = ((), (), s32[]{:S(2)}) async-start(), calls=%async_computation.2 | async-start | bytes 16515072 | tf_op jit(solution)/shard_map/reduce_scatter | solution.py:21
  120.1 145.7 %copy-start = (f32[64,7168]{1,0:T(8,128)S(1)}, f32[64,7168]{1,0:T(8,128)}, u32[]{:S(2)}) copy-start(f32[64,7168]{1,0:T(8,128)} %param.8) | copy-start | bytes 5505028
  120.2 150.6 %all-gather.8.cloned.1.call-start = ((), (), s32[]{:S(2)}) async-start(), calls=%async_computation.4 | async-start | bytes 1310720 | tf_op jit(solution)/shard_map/all_gather | solution.py:34
  120.7 222.9 %all-gather.6.cloned.1.call-start = ((), (), s32[]{:S(2)}) async-start(), calls=%async_computation.3 | async-start | bytes 8257536 | tf_op jit(solution)/shard_map/all_gather | solution.py:38
Sparse Core Ops, SparseCore 0:
  11.7 78.1 all-gather.3
  120.3 145.5 reduce-scatter.1
Sparse Core Ops, SparseCore 1:
  122.5 25.5 all-gather.7
  270.8 72.7 all-gather.5
where the time goes:
time: 400 us; the launch traced here: 396 us
  waiting for transfers between devices  300 us (75%)
  matrix products  46.2 us (12%)
  local copies, waits for them, and re-layouts  29.5 us (7%)
  between operations  15.5 us (4%)
  other arithmetic  4.84 us (1%)
    reduce_scatter x1, waiting for transfers between devices, per_device(): lax.psum_scatter(lax.dot_general(projected, out_grad, (((0,), (0,)), ((),...  145 us
    all_gather x1, waiting for transfers between devices, per_device(): lax.all_gather(projector, ('dp', 'tensor'), axis=0, tiled=True)  81.1 us
    all_gather x1, waiting for transfers between devices, per_device(): lax.all_gather(normalized, 'dp', axis=0, tiled=True)  72.8 us
    dot_general x1, matrix products, per_device(): lax.dot_general(projected, out_grad, (((0,), (0,)), ((), ())), preferred_...  30.3 us
    unnamed x3, local copies, waits for them, and re-layouts  29.5 us
    dot_general x1, matrix products, per_device(): jnp.dot(columns, lax.all_gather(normalized, 'dp', axis=0, tiled=True), pr...  15.9 us
  transfers between devices with their start and end apart: 4, of which 3 were waited for; matrix products, arithmetic and copies ran while one was open for 1% of the time, Pallas kernels for 0%

commit v1 on v0

v1 whole, which is shorter than its diff:
```python
import functools

import jax
import jax.numpy as jnp
from jax import lax
from jax.experimental import pallas as pl
from jax.experimental.pallas import tpu as pltpu
from jax.sharding import PartitionSpec as P

beta_one = 0.9
beta_two = 0.999
bias_one = 1.0 - 0.9**10
bias_two = 1.0 - 0.999**10
adam_eps = 1e-08

PARTS = 2
UNIT = 256
F32 = jnp.float32
BF16 = jnp.bfloat16
ANYWHERE = pl.BlockSpec(memory_space=pl.ANY)


def split_widths(columns):
    units, parts = columns // UNIT, min(PARTS, columns // UNIT)
    return [UNIT * (units // parts + (i < units % parts)) for i in range(parts)]


def params(mib):
    return pltpu.CompilerParams(vmem_limit_bytes=mib << 20)


def cost(flops, moved):
    return pl.CostEstimate(flops=flops, bytes_accessed=moved, transcendentals=0)


def gather(where, activations, many, depth):
    tokens = activations.shape[0]
    parts = max(1, 128 // depth)

    def body(where_ref, taken_ref, out_ref):
        for p in range(parts):

            @pl.when(where_ref[pl.program_id(0)] % parts == p)
            def _(p=p):
                out_ref[0] = taken_ref[:, p * depth : (p + 1) * depth]

    return pl.pallas_call(
        body,
        grid_spec=pltpu.PrefetchScalarGridSpec(
            num_scalar_prefetch=1,
            grid=(many,),
            in_specs=[pl.BlockSpec((tokens, parts * depth), lambda r, where: (0, where[r] // parts))],
            out_specs=pl.BlockSpec((1, tokens, depth), lambda r, where: (r, 0, 0)),
        ),
        out_shape=jax.ShapeDtypeStruct((many, tokens, depth), BF16),
        compiler_params=params(60),
        cost_estimate=cost(0, 4 * tokens * many * depth),
    )(where, activations)


def project(where, taken, slabs, tensor):
    tokens = taken.shape[1] // tensor
    depth, rank = slabs[0].shape
    many = len(slabs)

    def body(where_ref, taken_ref, *refs):
        held, outs = refs[:many], refs[many:]
        total = jnp.dot(taken_ref[0], held[0][...], preferred_element_type=F32)
        for r in range(1, many):
            total += jnp.dot(taken_ref[r], held[r][...], preferred_element_type=F32)
        for j in range(tensor):

            @pl.when(pl.program_id(0) == j)
            def _(j=j):
                outs[j][...] = total.astype(outs[j].dtype)

    whole = pl.BlockSpec((depth, rank), lambda j, where: (0, 0))
    out = pl.BlockSpec((tokens, rank), lambda j, where: (0, 0))
    return pl.pallas_call(
        body,
        grid_spec=pltpu.PrefetchScalarGridSpec(
            num_scalar_prefetch=1,
            grid=(tensor,),
            in_specs=[pl.BlockSpec((many, tokens, depth), lambda j, where: (0, where[j], 0))]
            + [whole] * many,
            out_specs=[out] * tensor,
        ),
        out_shape=[
            jax.ShapeDtypeStruct((tokens, rank), F32 if j == 0 else BF16) for j in range(tensor)
        ],
        compiler_params=params(32),
        cost_estimate=cost(
            2 * tensor * tokens * many * depth * rank, 2 * many * depth * (tensor * tokens + rank)
        ),
    )(where, taken, *slabs)


def flip(where, pieces, chips):
    tokens, rank = pieces[0].shape
    many = len(pieces)
    rows = rank // chips

    def body(where_ref, *refs):
        out = refs[many]
        for j in range(many):
            turned = refs[j][...].T
            at = pl.multiple_of(where_ref[j] * tokens, 128)
            refs[many + 1][...] = turned
            for i in range(chips):
                source = pl.multiple_of(where_ref[many + i] * rows, rows)
                out[pl.ds(i * rows, rows), pl.ds(at, tokens)] = refs[many + 1][pl.ds(source, rows), :]

    return pl.pallas_call(
        body,
        grid_spec=pltpu.PrefetchScalarGridSpec(
            num_scalar_prefetch=1,
            grid=(1,),
            in_specs=[pl.BlockSpec((tokens, rank), lambda i, where: (0, 0))] * many,
            out_specs=pl.BlockSpec((rank, many * tokens), lambda i, where: (0, 0)),
            scratch_shapes=[pltpu.VMEM((rank, tokens), BF16)],
        ),
        out_shape=jax.ShapeDtypeStruct((rank, many * tokens), BF16),
        compiler_params=params(16),
        cost_estimate=cost(0, 4 * rank * tokens * many),
    )(where, *pieces)


def arrange(where, pieces, choose):
    height, rank = pieces[0].shape
    many = len(pieces)

    def body(where_ref, choose_ref, *refs):
        for j in range(many):
            at = pl.multiple_of(where_ref[j] * height, height)
            refs[many][pl.ds(at, height), :] = jnp.dot(
                refs[j][...], choose_ref[...], preferred_element_type=F32
            ).astype(BF16)

    return pl.pallas_call(
        body,
        grid_spec=pltpu.PrefetchScalarGridSpec(
            num_scalar_prefetch=1,
            grid=(1,),
            in_specs=[pl.BlockSpec((rank, rank), lambda i, where: (0, 0))]
            + [pl.BlockSpec((height, rank), lambda i, where: (0, 0))] * many,
            out_specs=pl.BlockSpec((many * height, rank), lambda i, where: (0, 0)),
        ),
        out_shape=jax.ShapeDtypeStruct((many * height, rank), BF16),
        compiler_params=params(16),
        cost_estimate=cost(2 * rank * rank * height * many, 4 * rank * height * many),
    )(where, choose, *pieces)


def unset(shape):
    return pl.pallas_call(
        lambda out_ref: None,
        out_shape=jax.ShapeDtypeStruct(shape, F32),
        out_specs=ANYWHERE,
    )()


def per_device(dp, tensor, activations, out_grad, projector, first_moment, second_moment):
    chips = dp // 2
    dp_at, t_at = lax.axis_index("dp"), lax.axis_index("tensor")
    chip, core = dp_at // 2, dp_at % 2
    behind = jnp.where(core == 0, chip, chips - 1 - chip)
    slots = jnp.arange(chips)
    slot_chip = jnp.where(core == 0, chip + slots, chip - slots + chips) % chips
    peers = t_at ^ jnp.arange(tensor)
    columns = out_grad.shape[1]
    rank = projector.shape[1]
    rows = rank // chips

    def swap(value):
        return lax.ppermute(value, "dp", [(i, i ^ 1) for i in range(dp)])

    def rotate(value, by):
        pairs = [(2 * q + c, 2 * ((q + by) % chips) + c) for q in range(chips) for c in (0, 1)]
        return lax.ppermute(value, "dp", pairs)

    def onward(value):
        up = [(2 * q, 2 * q + 2) for q in range(chips - 1)]
        down = [(2 * q + 3, 2 * q + 1) for q in range(chips - 1)]
        return lax.ppermute(value, "dp", up + down)

    def exchange(value, j):
        return lax.ppermute(value, "tensor", [(t, t ^ j) for t in range(tensor)])

    state = {"last": None}

    def after(*values):
        if state["last"] is None:
            return values
        return lax.optimization_barrier((values, state["last"]))[0]

    def ended(value):
        state["last"] = value
        return value

    slabs = [projector] + [rotate(projector, chips - r) for r in range(1, chips)]
    order = (chip + slots) % chips * 2
    order = jnp.concatenate([order + core, order + 1 - core]) * tensor + t_at
    taken = ended(gather(order.astype(jnp.int32), activations, dp, projector.shape[0]))

    basis = [projector] + [exchange(projector, j) for j in range(1, tensor)]
    wanted = (slot_chip[:, None] * rows + jnp.arange(rows)[None]).reshape(-1)
    choose = (jnp.arange(rank)[:, None] == wanted[None]).astype(BF16)
    (choose,) = after(choose)
    basis = ended(arrange(peers.astype(jnp.int32), basis, choose))

    taken, *slabs[1:] = after(taken, *slabs[1:])
    slabs = slabs + [swap(slab) for slab in slabs]
    parts = project(peers.astype(jnp.int32), taken, slabs, tensor)
    ended(parts[0])
    total = parts[0]
    for j in range(1, tensor):
        total = total + exchange(parts[j], j).astype(F32)
    piece = total.astype(BF16)
    pieces = [piece] + [exchange(piece, j) for j in range(1, tensor)]
    flipped = flip(jnp.concatenate([peers, slot_chip]).astype(jnp.int32), pieces, chips)
    ended(flipped)

    widths = split_widths(columns)
    offsets = [sum(widths[:i]) for i in range(len(widths))]

    def cut(value, k):
        return lax.slice_in_dim(value, offsets[k], offsets[k] + widths[k], axis=1)

    def slot(value, i):
        return lax.slice_in_dim(value, i * rows, (i + 1) * rows, axis=0)

    state["update"] = unset((basis.shape[0], columns))
    state["new_first"], state["new_second"] = unset(first_moment.shape), unset(first_moment.shape)
    pending = []

    def put(name, value, k):
        state[name] = lax.dynamic_update_slice(state[name], value, (0, offsets[k]))

    def encode(k):
        weights, grad = after(flipped, out_grad)
        whole = jnp.dot(weights, cut(grad, k), preferred_element_type=F32).astype(BF16)
        ended(whole)
        return whole, swap(whole)

    def summed(whole, given, got, i, j):
        whole, given, *got = after(whole, given, *([] if got is None else [got]))
        total = slot(whole, i).astype(F32) + slot(given, j).astype(F32)
        for one in got:
            total = total + one.astype(F32)
        return total

    def adam(k, whole, given, got):
        whole, given, got = after(whole, given, got)
        other = swap(got)

        def own_half(value):
            return lax.dynamic_slice_in_dim(value, core * (rows // 2), rows // 2).astype(F32)

        total = own_half(slot(whole, 0)) + own_half(slot(given, 0)) + own_half(got) + own_half(other)
        new_first = beta_one * cut(first_moment, k) + (1.0 - beta_one) * total
        new_second = beta_two * cut(second_moment, k) + (1.0 - beta_two) * total * total
        step = new_first / bias_one / (jnp.sqrt(new_second / bias_two) + adam_eps)
        step = ended(step.astype(BF16))

        def moments():
            values = after(new_first, new_second)
            put("new_first", values[0], k)
            put("new_second", values[1], k)
            ended(state["new_second"])

        pending.append(moments)
        other = swap(step)
        return ended(
            jnp.concatenate([jnp.where(core == 0, step, other), jnp.where(core == 0, other, step)])
        )

    def decode(k, step, arrived, passed):
        step, *values = after(step, *arrived, *passed)
        arrived, passed = values[: chips - 1], values[chips - 1 :]
        pieces = [step] + [
            jnp.where(behind >= chips - i, arrived[chips - 1 - i], passed[i - 1])
            for i in range(1, chips)
        ]
        put("update", jnp.dot(basis, jnp.concatenate(pieces), preferred_element_type=F32), k)
        ended(state["update"])

    def stream(ks):
        before, ahead = None, None
        for k in [*ks, None]:
            if k is not None:
                whole, given = encode(k) if ahead is None else ahead.pop()
                if before is None:
                    yield
                if k != ks[-1]:
                    ahead = []
                    pending.append(lambda ahead=ahead, k=k: ahead.append(encode(ks[ks.index(k) + 1])))
            got = None
            for step in range(chips - 1 if k is not None else chips - 2):
                forward = before is not None and step < chips - 2
                if k is not None:
                    i = chips - 1 - step
                    send = summed(whole, given, got, i, chips - i).astype(BF16)
                    if forward:
                        send = jnp.where(behind <= step, send, before[2][-1])
                    ended(send)
                else:
                    send = before[2][-1]
                got = onward(send)
                if forward:
                    prior, own, arrived, passed = before
                    arrived.append(got)
                    passed.append(swap(*after(got)))
                    if step == chips - 3:
                        pending.append(functools.partial(decode, prior, own, arrived, passed))
                yield
            if k is None:
                return
            own = adam(k, whole, given, got)
            got = onward(own)
            before = (k, own, [got], [swap(got)])
            yield

    running = [stream(list(range(n, len(widths), 2))) for n in range(min(2, len(widths)))]
    started = 0
    while running:
        for one in list(running):
            if next(one, running) is running:
                running.remove(one)
            elif pending and started >= 2:
                pending.pop(0)()
            started += 1
    while pending:
        pending.pop(0)()
    return state["update"], state["new_first"], state["new_second"]


def solution(mesh):
    in_specs = (
        P("dp", None),
        P("dp", "tensor"),
        P(("dp", "tensor"), None),
        P("dp", "tensor"),
        P("dp", "tensor"),
    )
    out_specs = (P("dp", "tensor"), P("dp", "tensor"), P("dp", "tensor"))
    return jax.shard_map(
        functools.partial(per_device, mesh.shape["dp"], mesh.shape["tensor"]),
        mesh=mesh,
        in_specs=in_specs,
        out_specs=out_specs,
        check_vma=False,
    )
```

time: 400 us -> 248 us (0.62)
  waiting for transfers between devices: 300 us -> 141 us
  starting transfers between devices: 0.34 us -> 42.1 us
  local copies, waits for them, and re-layouts: 29.5 us -> 6.6 us
  matrix products: 46.2 us -> 27 us
  between operations: 15.5 us -> 1.25 us
  Pallas kernels: 0 us -> 13.4 us
  other arithmetic: 4.84 us -> 15.3 us
    all_gather x3 -> x0, waiting for transfers between devices: 154 us -> none  [the longest x1 81.1 us: per_device(): lax.all_gather(projector, ('dp', 'tensor'), axis=0, tiled=True)]
    reduce_scatter x1 -> x0, waiting for transfers between devices: 145 us -> none  [per_device(): lax.psum_scatter(lax.dot_general(projected, out_grad, (((0,), (0,)), ((),...]
    ppermute x0 -> x40, waiting for transfers between devices: none -> 141 us  [the longest x12 99.2 us: onward(): return lax.ppermute(value, 'dp', up + down)]
    ppermute x0 -> x40, starting transfers between devices: none -> 42.1 us  [the longest x12 23.3 us: onward(): return lax.ppermute(value, 'dp', up + down)]
    unnamed x3 -> x42, local copies, waits for them, and re-layouts: 29.5 us -> 3.5 us
    dot_general x2 -> x4, matrix products: 46.2 us -> 27 us  [the longest x2 15.1 us: decode(): jnp.dot(basis, jnp.concatenate(pieces), preferred_element_type=F32)]
    pallas_call x0 -> x7, Pallas kernels: none -> 13.4 us  [the longest x1 7.41 us: gather(): pl.pallas_call(body, grid_spec=pltpu.PrefetchScalarGridSpec(num_scalar_pr...]
    select_n x0 -> x8, other arithmetic: none -> 7.68 us  [the longest x6 6.53 us: decode(): jnp.where(behind >= chips - i, arrived[chips - 1 - i], passed[i - 1])]
  transfers between devices with their start and end apart: 4 -> 40, of which waited for: 3 -> 27; matrix products, arithmetic and copies ran while one was open for 1% -> 10% of each run, Pallas kernels for 0% -> 4%
where the time goes in v1:
time: 248 us; the launch traced here: 247 us
  waiting for transfers between devices  141 us (57%)
  starting transfers between devices  42.1 us (17%)
  matrix products  27 us (11%)
  other arithmetic  15.3 us (6%)
  Pallas kernels  13.4 us (5%)
  local copies, waits for them, and re-layouts  6.6 us (3%)
    ppermute x12, waiting for transfers between devices, onward(): return lax.ppermute(value, 'dp', up + down)  99.2 us
    ppermute x9, waiting for transfers between devices, exchange(): return lax.ppermute(value, 'tensor', [(t, t ^ j) for t in range(tensor)])  23.9 us
    ppermute x12, starting transfers between devices, onward(): return lax.ppermute(value, 'dp', up + down)  23.3 us
    dot_general x2, matrix products, decode(): jnp.dot(basis, jnp.concatenate(pieces), preferred_element_type=F32)  15.1 us
    dot_general x2, matrix products, encode(): jnp.dot(weights, cut(grad, k), preferred_element_type=F32).astype(BF16)  11.9 us
    ppermute x9, starting transfers between devices, exchange(): return lax.ppermute(value, 'tensor', [(t, t ^ j) for t in range(tensor)])  10.7 us
    ppermute x16, waiting for transfers between devices, swap(): return lax.ppermute(value, 'dp', [(i, i ^ 1) for i in range(dp)])  9.7 us
    ppermute x3, waiting for transfers between devices, rotate(): return lax.ppermute(value, 'dp', pairs)  8.61 us
  transfers between devices with their start and end apart: 40, of which 27 were waited for; matrix products, arithmetic and copies ran while one was open for 10% of the time, Pallas kernels for 4%

profile of v1, /device:TPU:16, one launch (start us, length us, event | category | flops | bytes accessed | tf_op | source)
XLA Modules:
  0.0 247.1 jit_solution(2834215140823378731)
XLA Ops:
  0.6 1.6 collective-permute-start
  2.2 1.5 collective-permute-start.1
  4.6 3.5 %collective-permute-start.4 = (bf16[256,512]{1,0:T(8,128)(2,1)}, bf16[256,512]{1,0:T(8,128)(2,1)S(1)}, u32[]{:S(2)}, u32[]{:S(2)}) collective-permute-start(bf16[256,512]{1,0:T(8,128)(2,1)} %refs_0_.3), channel_id=1, source_target_pairs={{0,16},{4,20},{8,24},{12,28},{16,0},{20,4},{24,8},{28,12},{1,17},{... | collective-permute-start | bytes 786440 | tf_op jit(solution)/shard_map/ppermute | solution.py:179
  8.4 1.7 collective-permute-done.refs_1_
  10.1 1.6 collective-permute-start.5
  12.3 7.4 %shard_map.77.taken_ref = bf16[8,1024,256]{2,1,0:T(8,128)(2,1)} custom-call(s32[8]{0:T(128)} %fusion.30.where_ref, bf16[1024,8192]{1,0:T(8,128)(2,1)} %taken_ref.1), custom_call_target="tpu_custom_call" | custom-call | bytes 8388608 | tf_op jit(solution)/shard_map/pallas_call | solution.py:47
  19.8 1.2 shard_map.78
  21.0 1.9 collective-permute-done.3.refs_1_
  23.0 3.6 %collective-permute-done.4.refs_2_ = bf16[256,512]{1,0:T(8,128)(2,1)S(1)} collective-permute-done((bf16[256,512]{1,0:T(8,128)(2,1)}, bf16[256,512]{1,0:T(8,128)(2,1)S(1)}, u32[]{:S(2)}, u32[]{:S(2)}) %collective-permute-start.4) | collective-permute-done | bytes 262176 | tf_op jit(solution)/shard_map/ppermute | solution.py:179
  26.5 3.1 %collective-permute-done.5.refs_3_ = bf16[256,512]{1,0:T(8,128)(2,1)S(1)} collective-permute-done((bf16[256,512]{1,0:T(8,128)(2,1)}, bf16[256,512]{1,0:T(8,128)(2,1)S(1)}, u32[]{:S(2)}, u32[]{:S(2)}) %collective-permute-start.5) | collective-permute-done | bytes 262176 | tf_op jit(solution)/shard_map/ppermute | solution.py:179
  30.2 1.0 collective-permute-done.7.refs_5_
  31.9 2.2 copy-done
  34.1 3.8 %shard_map.79 = (f32[256,512]{1,0:T(8,128)S(1)}, bf16[256,512]{1,0:T(8,128)(2,1)S(1)}, bf16[256,512]{1,0:T(8,128)(2,1)S(1)}, bf16[256,512]{1,0:T(8,128)(2,1)S(1)}) custom-call(s32[4]{0:T(128)S(1)} %iota_xor_fusion.where_ref, bf16[8,1024,256]{2,1,0:T(8,128)(2,1)S(1)} %copy-done, bf16[256,512]{1,0:T(8,128)(2,1)S(1)} %copy-done.1, ...), custom_call_target="tpu_custom_call" | custom-call | flops 2147483648 | bytes 6291456 | tf_op jit(solution)/shard_map/pallas_call | solution.py:79
  38.0 1.6 collective-permute-start.10
  39.5 1.5 collective-permute-start.11
  41.5 5.7 %collective-permute-done.10 = bf16[256,512]{1,0:T(8,128)(2,1)S(1)} collective-permute-done((bf16[256,512]{1,0:T(8,128)(2,1)S(1)}, bf16[256,512]{1,0:T(8,128)(2,1)S(1)}, u32[]{:S(2)}, u32[]{:S(2)}) %collective-permute-start.10) | collective-permute-done | bytes 262176 | tf_op jit(solution)/shard_map/ppermute | solution.py:187
  47.2 6.0 %collective-permute-done.11 = bf16[256,512]{1,0:T(8,128)(2,1)S(1)} collective-permute-done((bf16[256,512]{1,0:T(8,128)(2,1)S(1)}, bf16[256,512]{1,0:T(8,128)(2,1)S(1)}, u32[]{:S(2)}, u32[]{:S(2)}) %collective-permute-start.11) | collective-permute-done | bytes 262176 | tf_op jit(solution)/shard_map/ppermute | solution.py:187
  53.4 1.3 collective-permute-start.13
  55.5 1.4 collective-permute-start.15
  57.0 5.7 %collective-permute-done.13.refs_1_ = bf16[256,512]{1,0:T(8,128)(2,1)S(1)} collective-permute-done((bf16[256,512]{1,0:T(8,128)(2,1)S(1)}, bf16[256,512]{1,0:T(8,128)(2,1)S(1)}, u32[]{:S(2)}, u32[]{:S(2)}) %collective-permute-start.13) | collective-permute-done | bytes 262176 | tf_op jit(solution)/shard_map/ppermute | solution.py:187
  62.7 4.8 %collective-permute-done.14.refs_2_ = bf16[256,512]{1,0:T(8,128)(2,1)S(1)} collective-permute-done((bf16[256,512]{1,0:T(8,128)(2,1)S(1)}, bf16[256,512]{1,0:T(8,128)(2,1)S(1)}, u32[]{:S(2)}, u32[]{:S(2)}) %collective-permute-start.14) | collective-permute-done | bytes 262176 | tf_op jit(solution)/shard_map/ppermute | solution.py:187
  68.5 7.6 %fusion.4 = bf16[512,3584]{1,0:T(8,128)(2,1)S(1)} fusion(bf16[512,1024]{1,0:T(8,128)(2,1)S(1)} %shard_map.80, bf16[1024,7168]{1,0:T(8,128)(2,1)} %param.6), kind=kOutput, calls=%fused_computation.6 | convolution fusion | flops 3759931392 | bytes 12058624 | tf_op jit(solution)/shard_map/dot_general | solution.py:241
  76.3 4.3 %fusion.7 = bf16[512,3584]{1,0:T(8,128)(2,1)S(1)} fusion(bf16[512,1024]{1,0:T(8,128)(2,1)S(1)} %shard_map.80, bf16[1024,7168]{1,0:T(8,128)(2,1)S(1)} %bitcast.7), kind=kOutput, calls=%fused_computation.7 | convolution fusion | flops 3759931392 | bytes 12058624 | tf_op jit(solution)/shard_map/dot_general | solution.py:241
  81.1 1.5 collective-permute-done.16
  82.8 1.9 collective-permute-start.17
  84.8 3.1 %collective-permute-done.18 = bf16[512,3584]{1,0:T(8,128)(2,1)S(1)} collective-permute-done((bf16[512,3584]{1,0:T(8,128)(2,1)S(1)}, bf16[512,3584]{1,0:T(8,128)(2,1)S(1)}, u32[]{:S(2)}, u32[]{:S(2)}) %collective-permute-start.18) | collective-permute-done | bytes 3670048 | tf_op jit(solution)/shard_map/ppermute | solution.py:175
  88.2 1.9 collective-permute-start.20
  90.1 8.0 %collective-permute-done.17 = bf16[128,3584]{1,0:T(8,128)(2,1)S(1)} collective-permute-done((bf16[128,3584]{1,0:T(8,128)(2,1)S(1)}, bf16[128,3584]{1,0:T(8,128)(2,1)S(1)}, u32[]{:S(2)}, u32[]{:S(2)}) %collective-permute-start.17) | collective-permute-done | bytes 917536 | tf_op jit(solution)/shard_map/ppermute | solution.py:184
  98.5 1.9 collective-permute-start.19
  100.5 7.5 %collective-permute-done.20 = bf16[128,3584]{1,0:T(8,128)(2,1)S(1)} collective-permute-done((bf16[128,3584]{1,0:T(8,128)(2,1)S(1)}, bf16[128,3584]{1,0:T(8,128)(2,1)S(1)}, u32[]{:S(2)}, u32[]{:S(2)}) %collective-permute-start.20) | collective-permute-done | bytes 917536 | tf_op jit(solution)/shard_map/ppermute | solution.py:184
  108.3 1.9 collective-permute-start.22
  110.3 7.5 %collective-permute-done.19 = bf16[128,3584]{1,0:T(8,128)(2,1)S(1)} collective-permute-done((bf16[128,3584]{1,0:T(8,128)(2,1)S(1)}, bf16[128,3584]{1,0:T(8,128)(2,1)S(1)}, u32[]{:S(2)}, u32[]{:S(2)}) %collective-permute-start.19) | collective-permute-done | bytes 917536 | tf_op jit(solution)/shard_map/ppermute | solution.py:184
  118.2 1.9 collective-permute-start.21
  120.1 7.5 %collective-permute-done.22 = bf16[128,3584]{1,0:T(8,128)(2,1)S(1)} collective-permute-done((bf16[128,3584]{1,0:T(8,128)(2,1)S(1)}, bf16[128,3584]{1,0:T(8,128)(2,1)S(1)}, u32[]{:S(2)}, u32[]{:S(2)}) %collective-permute-start.22) | collective-permute-done | bytes 917536 | tf_op jit(solution)/shard_map/ppermute | solution.py:184
  127.6 1.3 add_convert_fusion
  128.9 8.5 %collective-permute-done.21 = bf16[128,3584]{1,0:T(8,128)(2,1)S(1)} collective-permute-done((bf16[128,3584]{1,0:T(8,128)(2,1)S(1)}, bf16[128,3584]{1,0:T(8,128)(2,1)S(1)}, u32[]{:S(2)}, u32[]{:S(2)}) %collective-permute-start.21) | collective-permute-done | bytes 917536 | tf_op jit(solution)/shard_map/ppermute | solution.py:184
  137.5 1.6 slice.81
  139.1 1.0 collective-permute-done.23
  140.1 2.5 %divide_convert_fusion.1 = (bf16[64,3584]{1,0:T(8,128)(2,1)S(1)}, f32[64,3584]{1,0:T(8,128)S(1)}, f32[64,3584]{1,0:T(8,128)S(1)}) fusion(bf16[128,3584]{1,0:T(8,128)(2,1)} %collective-permute-done.23, s32[]{:T(128)S(6)} %select_n.109, bf16[128,3584]{1,0:T(8,128)(2,1)} %copy-done.16, bf16[128,3584]{1,0:T(8,128)(2,1)S(1)} %slice-done.1, ...), kind=kLoop, calls=%fused_computation.39 | loop fusion | flops 4358144 | bytes 5963780 | tf_op jit(solution)/shard_map/convert_element_type | solution.py:263
  142.8 2.0 collective-permute-start.29
  144.9 1.1 broadcast_select_fusion.9
  146.1 12.3 %collective-permute-done.29 = bf16[128,3584]{1,0:T(8,128)(2,1)S(1)} collective-permute-done((bf16[128,3584]{1,0:T(8,128)(2,1)}, bf16[128,3584]{1,0:T(8,128)(2,1)S(1)}, u32[]{:S(2)}, u32[]{:S(2)}) %collective-permute-start.29) | collective-permute-done | bytes 917536 | tf_op jit(solution)/shard_map/ppermute | solution.py:184
  158.4 2.1 collective-permute-start.25
  160.5 1.2 slice.85
  163.2 10.6 %collective-permute-done.25 = bf16[128,3584]{1,0:T(8,128)(2,1)} collective-permute-done((bf16[128,3584]{1,0:T(8,128)(2,1)S(1)}, bf16[128,3584]{1,0:T(8,128)(2,1)}, u32[]{:S(2)}, u32[]{:S(2)}) %collective-permute-start.25) | collective-permute-done | bytes 917536 | tf_op jit(solution)/shard_map/ppermute | solution.py:184
  173.8 1.9 collective-permute-start.26
  175.9 1.9 collective-permute-start.34
  177.8 11.6 %collective-permute-done.26 = bf16[128,3584]{1,0:T(8,128)(2,1)} collective-permute-done((bf16[128,3584]{1,0:T(8,128)(2,1)}, bf16[128,3584]{1,0:T(8,128)(2,1)}, u32[]{:S(2)}, u32[]{:S(2)}) %collective-permute-start.26) | collective-permute-done | bytes 917536 | tf_op jit(solution)/shard_map/ppermute | solution.py:184
  189.4 1.9 collective-permute-start.27
  191.5 1.2 copy-done.11
  192.7 6.5 %collective-permute-done.34 = bf16[128,3584]{1,0:T(8,128)(2,1)} collective-permute-done((bf16[128,3584]{1,0:T(8,128)(2,1)S(1)}, bf16[128,3584]{1,0:T(8,128)(2,1)}, u32[]{:S(2)}, u32[]{:S(2)}) %collective-permute-start.34) | collective-permute-done | bytes 917536 | tf_op jit(solution)/shard_map/ppermute | solution.py:184
  199.2 1.9 collective-permute-start.35
  201.2 7.8 %collective-permute-done.27 = bf16[128,3584]{1,0:T(8,128)(2,1)} collective-permute-done((bf16[128,3584]{1,0:T(8,128)(2,1)}, bf16[128,3584]{1,0:T(8,128)(2,1)}, u32[]{:S(2)}, u32[]{:S(2)}) %collective-permute-start.27) | collective-permute-done | bytes 917536 | tf_op jit(solution)/shard_map/ppermute | solution.py:184
  209.6 9.3 %collective-permute-done.35 = bf16[128,3584]{1,0:T(8,128)(2,1)} collective-permute-done((bf16[128,3584]{1,0:T(8,128)(2,1)}, bf16[128,3584]{1,0:T(8,128)(2,1)}, u32[]{:S(2)}, u32[]{:S(2)}) %collective-permute-start.35) | collective-permute-done | bytes 917536 | tf_op jit(solution)/shard_map/ppermute | solution.py:184
  218.9 1.9 collective-permute-start.36
  220.8 1.3 broadcast_select_fusion.5
  222.1 1.3 broadcast_select_fusion.3
  223.4 1.3 broadcast_select_fusion.1
  224.7 7.6 %convolution_dynamic-update-slice_fusion.1 = f32[1024,7168]{1,0:T(8,128)} fusion(f32[1024,7168]{1,0:T(8,128)} %shard_map.76, bf16[1024,512]{1,0:T(8,128)(2,1)S(1)} %shard_map.78, bf16[128,3584]{1,0:T(8,128)(2,1)S(1)} %broadcast_select_fusion.1, bf16[128,3584]{1,0:T(8,128)(2,1)S(1)} %broadcast_select_fusion.3, ...), kind=kOutput, calls=%fused_computation.1 | convolution fusion | flops 3772776448 | bytes 19398656 | tf_op jit(solution)/shard_map/dot_general | solution.py:284
  232.3 2.1 collective-permute-done.36
  234.6 2.3 collective-permute-done.39
  237.0 1.3 broadcast_select_fusion.2
  238.2 1.3 broadcast_select_fusion
  239.6 7.6 %convolution_dynamic-update-slice_fusion = f32[1024,7168]{1,0:T(8,128)} fusion(f32[1024,7168]{1,0:T(8,128)} %convolution_dynamic-update-slice_fusion.1, bf16[1024,512]{1,0:T(8,128)(2,1)S(1)} %shard_map.78, bf16[128,3584]{1,0:T(8,128)(2,1)S(1)} %broadcast_select_fusion, bf16[128,3584]{1,0:T(8,128)(2,1)S(1)} %broadcast_select_fusion.2, ...), kind=kOutput, calls=%fused_computation | convolution fusion | flops 3772776448 | bytes 19398656 | tf_op jit(solution)/shard_map/dot_general | solution.py:284
  (106 shorter events, 10.8 us)
Async XLA Ops:
  0.6 9.5 %collective-permute-start = (bf16[256,512]{1,0:T(8,128)(2,1)}, bf16[256,512]{1,0:T(8,128)(2,1)S(1)}, u32[]{:S(2)}, u32[]{:S(2)}) collective-permute-start(bf16[256,512]{1,0:T(8,128)(2,1)} %refs_0_.3), channel_id=1, source_target_pairs={{0,1},{1,0},{2,3},{3,2},{4,5},{5,4},{6,7},{7,6},{8,9},{9,8},{10,11... | collective-permute-start | bytes 786440 | tf_op jit(solution)/shard_map/ppermute | solution.py:187
  2.2 17.5 %collective-permute-start.1 = (bf16[256,512]{1,0:T(8,128)(2,1)}, bf16[256,512]{1,0:T(8,128)(2,1)S(1)}, u32[]{:S(2)}, u32[]{:S(2)}) collective-permute-start(bf16[256,512]{1,0:T(8,128)(2,1)} %refs_0_.3), channel_id=1, source_target_pairs={{0,2},{1,3},{2,0},{3,1},{4,6},{5,7},{6,4},{7,5},{8,10},{9,11},{10,... | collective-permute-start | bytes 786440 | tf_op jit(solution)/shard_map/ppermute | solution.py:187
  3.7 16.1 %collective-permute-start.2 = (bf16[256,512]{1,0:T(8,128)(2,1)}, bf16[256,512]{1,0:T(8,128)(2,1)S(1)}, u32[]{:S(2)}, u32[]{:S(2)}) collective-permute-start(bf16[256,512]{1,0:T(8,128)(2,1)} %refs_0_.3), channel_id=1, source_target_pairs={{0,3},{1,2},{2,1},{3,0},{4,7},{5,6},{6,5},{7,4},{8,11},{9,10},{10,... | collective-permute-start | bytes 786440 | tf_op jit(solution)/shard_map/ppermute | solution.py:187
  4.2 18.8 %collective-permute-start.3 = (bf16[256,512]{1,0:T(8,128)(2,1)}, bf16[256,512]{1,0:T(8,128)(2,1)S(1)}, u32[]{:S(2)}, u32[]{:S(2)}) collective-permute-start(bf16[256,512]{1,0:T(8,128)(2,1)} %refs_0_.3), channel_id=1, source_target_pairs={{0,24},{4,28},{8,0},{12,4},{16,8},{20,12},{24,16},{28,20},{1,25},{... | collective-permute-start | bytes 786440 | tf_op jit(solution)/shard_map/ppermute | solution.py:179
  4.6 21.9 %collective-permute-start.4 = (bf16[256,512]{1,0:T(8,128)(2,1)}, bf16[256,512]{1,0:T(8,128)(2,1)S(1)}, u32[]{:S(2)}, u32[]{:S(2)}) collective-permute-start(bf16[256,512]{1,0:T(8,128)(2,1)} %refs_0_.3), channel_id=1, source_target_pairs={{0,16},{4,20},{8,24},{12,28},{16,0},{20,4},{24,8},{28,12},{1,17},{... | collective-permute-start | bytes 786440 | tf_op jit(solution)/shard_map/ppermute | solution.py:179
  10.1 19.5 %collective-permute-start.5 = (bf16[256,512]{1,0:T(8,128)(2,1)}, bf16[256,512]{1,0:T(8,128)(2,1)S(1)}, u32[]{:S(2)}, u32[]{:S(2)}) collective-permute-start(bf16[256,512]{1,0:T(8,128)(2,1)} %refs_0_.3), channel_id=1, source_target_pairs={{0,8},{4,12},{8,16},{12,20},{16,24},{20,28},{24,0},{28,4},{1,9},{5... | collective-permute-start | bytes 786440 | tf_op jit(solution)/shard_map/ppermute | solution.py:179
  12.3 7.4 %copy-start.1 = (bf16[256,512]{1,0:T(8,128)(2,1)S(1)}, bf16[256,512]{1,0:T(8,128)(2,1)}, u32[]{:S(2)}) copy-start(bf16[256,512]{1,0:T(8,128)(2,1)} %refs_0_.3) | copy-start | bytes 786436
  19.7 10.5 %collective-permute-start.6 = (bf16[256,512]{1,0:T(8,128)(2,1)S(1)}, bf16[256,512]{1,0:T(8,128)(2,1)S(1)}, u32[]{:S(2)}, u32[]{:S(2)}) collective-permute-start(bf16[256,512]{1,0:T(8,128)(2,1)S(1)} %copy-done.1), channel_id=1, source_target_pairs={{0,4},{4,0},{8,12},{12,8},{16,20},{20,16},{24,28},{28,24},{1,5},{5... | collective-permute-start | bytes 786440 | tf_op jit(solution)/shard_map/ppermute | solution.py:175
  29.6 1.5 collective-permute-start.7
  29.6 1.9 collective-permute-start.8
  30.1 1.8 collective-permute-start.9
  31.9 2.2 copy-start
  38.0 9.2 %collective-permute-start.10 = (bf16[256,512]{1,0:T(8,128)(2,1)S(1)}, bf16[256,512]{1,0:T(8,128)(2,1)S(1)}, u32[]{:S(2)}, u32[]{:S(2)}) collective-permute-start(bf16[256,512]{1,0:T(8,128)(2,1)S(1)} %get-tuple-element.66), channel_id=1, source_target_pairs={{0,1},{1,0},{2,3},{3,2},{4,5},{5,4},{6,7},{7,6},{8,9},{9,8},{10,11... | collective-permute-start | bytes 786440 | tf_op jit(solution)/shard_map/ppermute | solution.py:187
  39.5 13.7 %collective-permute-start.11 = (bf16[256,512]{1,0:T(8,128)(2,1)S(1)}, bf16[256,512]{1,0:T(8,128)(2,1)S(1)}, u32[]{:S(2)}, u32[]{:S(2)}) collective-permute-start(bf16[256,512]{1,0:T(8,128)(2,1)S(1)} %get-tuple-element.67), channel_id=1, source_target_pairs={{0,2},{1,3},{2,0},{3,1},{4,6},{5,7},{6,4},{7,5},{8,10},{9,11},{10,... | collective-permute-start | bytes 786440 | tf_op jit(solution)/shard_map/ppermute | solution.py:187
  41.0 12.2 %collective-permute-start.12 = (bf16[256,512]{1,0:T(8,128)(2,1)S(1)}, bf16[256,512]{1,0:T(8,128)(2,1)S(1)}, u32[]{:S(2)}, u32[]{:S(2)}) collective-permute-start(bf16[256,512]{1,0:T(8,128)(2,1)S(1)} %get-tuple-element.68), channel_id=1, source_target_pairs={{0,3},{1,2},{2,1},{3,0},{4,7},{5,6},{6,5},{7,4},{8,11},{9,10},{10,... | collective-permute-start | bytes 786440 | tf_op jit(solution)/shard_map/ppermute | solution.py:187
  53.4 9.3 %collective-permute-start.13 = (bf16[256,512]{1,0:T(8,128)(2,1)S(1)}, bf16[256,512]{1,0:T(8,128)(2,1)S(1)}, u32[]{:S(2)}, u32[]{:S(2)}) collective-permute-start(bf16[256,512]{1,0:T(8,128)(2,1)S(1)} %add_convert_fusion.6.refs_0_), channel_id=1, source_target_pairs={{0,1},{1,0},{2,3},{3,2},{4,5},{5,4},{6,7},{7,6},{8,9},{9,8},{10,11... | collective-permute-start | bytes 786440 | tf_op jit(solution)/shard_map/ppermute | solution.py:187
  54.7 12.9 %collective-permute-start.14 = (bf16[256,512]{1,0:T(8,128)(2,1)S(1)}, bf16[256,512]{1,0:T(8,128)(2,1)S(1)}, u32[]{:S(2)}, u32[]{:S(2)}) collective-permute-start(bf16[256,512]{1,0:T(8,128)(2,1)S(1)} %add_convert_fusion.6.refs_0_), channel_id=1, source_target_pairs={{0,2},{1,3},{2,0},{3,1},{4,6},{5,7},{6,4},{7,5},{8,10},{9,11},{10,... | collective-permute-start | bytes 786440 | tf_op jit(solution)/shard_map/ppermute | solution.py:187
  55.5 12.0 %collective-permute-start.15 = (bf16[256,512]{1,0:T(8,128)(2,1)S(1)}, bf16[256,512]{1,0:T(8,128)(2,1)S(1)}, u32[]{:S(2)}, u32[]{:S(2)}) collective-permute-start(bf16[256,512]{1,0:T(8,128)(2,1)S(1)} %add_convert_fusion.6.refs_0_), channel_id=1, source_target_pairs={{0,3},{1,2},{2,1},{3,0},{4,7},{5,6},{6,5},{7,4},{8,11},{9,10},{10,... | collective-permute-start | bytes 786440 | tf_op jit(solution)/shard_map/ppermute | solution.py:187
  67.5 8.7 %slice-start.2 = ((s8[14680064]{0:T(1024)(128)(4,1)}), s8[4194304]{0:T(1024)(128)(4,1)S(1)}, s32[]{:S(2)}) async-start(s8[14680064]{0:T(1024)(128)(4,1)} %bitcast.6), calls=%async_computation.2 | async-start | bytes 8388608
  68.5 7.8 %slice-start.3 = ((s8[14680064]{0:T(1024)(128)(4,1)}), s8[4194304]{0:T(1024)(128)(4,1)S(1)}, s32[]{:S(2)}) async-start(s8[14680064]{0:T(1024)(128)(4,1)} %bitcast.6), calls=%async_computation.3 | async-start | bytes 8388608
  68.5 7.8 %slice-start.4 = ((s8[14680064]{0:T(1024)(128)(4,1)}), s8[4194304]{0:T(1024)(128)(4,1)S(1)}, s32[]{:S(2)}) async-start(s8[14680064]{0:T(1024)(128)(4,1)} %bitcast.6), calls=%async_computation.4 | async-start | bytes 8388608
  68.5 7.7 %slice-start.5 = ((s8[14680064]{0:T(1024)(128)(4,1)}), s8[2097152]{0:T(1024)(128)(4,1)S(1)}, s32[]{:S(2)}) async-start(s8[14680064]{0:T(1024)(128)(4,1)} %bitcast.6), calls=%async_computation.5 | async-start | bytes 4194304
  76.1 41.7 %copy-start.4 = (bf16[512,3584]{1,0:T(8,128)(2,1)}, bf16[512,3584]{1,0:T(8,128)(2,1)S(1)}, u32[]{:S(2)}) copy-start(bf16[512,3584]{1,0:T(8,128)(2,1)S(1)} %fusion.4) | copy-start | bytes 11010052
  76.1 6.5 %collective-permute-start.16 = (bf16[512,3584]{1,0:T(8,128)(2,1)S(1)}, bf16[512,3584]{1,0:T(8,128)(2,1)S(1)}, u32[]{:S(2)}, u32[]{:S(2)}) collective-permute-start(bf16[512,3584]{1,0:T(8,128)(2,1)S(1)} %fusion.4), channel_id=1, source_target_pairs={{0,4},{4,0},{8,12},{12,8},{16,20},{20,16},{24,28},{28,24},{1,5},{5... | collective-permute-start | bytes 11010056 | tf_op jit(solution)/shard_map/ppermute | solution.py:175
  80.5 47.1 %copy-start.2 = (bf16[512,3584]{1,0:T(8,128)(2,1)}, bf16[512,3584]{1,0:T(8,128)(2,1)S(1)}, u32[]{:S(2)}) copy-start(bf16[512,3584]{1,0:T(8,128)(2,1)S(1)} %fusion.7) | copy-start | bytes 11010052
  80.6 7.3 %collective-permute-start.18 = (bf16[512,3584]{1,0:T(8,128)(2,1)S(1)}, bf16[512,3584]{1,0:T(8,128)(2,1)S(1)}, u32[]{:S(2)}, u32[]{:S(2)}) collective-permute-start(bf16[512,3584]{1,0:T(8,128)(2,1)S(1)} %fusion.7), channel_id=1, source_target_pairs={{0,4},{4,0},{8,12},{12,8},{16,20},{20,16},{24,28},{28,24},{1,5},{5... | collective-permute-start | bytes 11010056 | tf_op jit(solution)/shard_map/ppermute | solution.py:175
  82.6 35.2 %copy-start.5 = (bf16[512,3584]{1,0:T(8,128)(2,1)}, bf16[512,3584]{1,0:T(8,128)(2,1)S(1)}, u32[]{:S(2)}) copy-start(bf16[512,3584]{1,0:T(8,128)(2,1)S(1)} %collective-permute-done.16) | copy-start | bytes 11010052
  82.8 15.3 %collective-permute-start.17 = (bf16[128,3584]{1,0:T(8,128)(2,1)S(1)}, bf16[128,3584]{1,0:T(8,128)(2,1)S(1)}, u32[]{:S(2)}, u32[]{:S(2)}) collective-permute-start(bf16[128,3584]{1,0:T(8,128)(2,1)S(1)} %add_convert_fusion.5), channel_id=1, source_target_pairs={{0,8},{8,16},{16,24},{12,4},{20,12},{28,20},{1,9},{9,17},{17,25},{... | collective-permute-start | bytes 2752520 | tf_op jit(solution)/shard_map/ppermute | solution.py:184
  87.9 39.8 %copy-start.3 = (bf16[512,3584]{1,0:T(8,128)(2,1)}, bf16[512,3584]{1,0:T(8,128)(2,1)S(1)}, u32[]{:S(2)}) copy-start(bf16[512,3584]{1,0:T(8,128)(2,1)S(1)} %collective-permute-done.18) | copy-start | bytes 11010052
  88.2 19.8 %collective-permute-start.20 = (bf16[128,3584]{1,0:T(8,128)(2,1)S(1)}, bf16[128,3584]{1,0:T(8,128)(2,1)S(1)}, u32[]{:S(2)}, u32[]{:S(2)}) collective-permute-start(bf16[128,3584]{1,0:T(8,128)(2,1)S(1)} %add_convert_fusion.4), channel_id=1, source_target_pairs={{0,8},{8,16},{16,24},{12,4},{20,12},{28,20},{1,9},{9,17},{17,25},{... | collective-permute-start | bytes 2752520 | tf_op jit(solution)/shard_map/ppermute | solution.py:184
  98.5 19.2 %collective-permute-start.19 = (bf16[128,3584]{1,0:T(8,128)(2,1)S(1)}, bf16[128,3584]{1,0:T(8,128)(2,1)S(1)}, u32[]{:S(2)}, u32[]{:S(2)}) collective-permute-start(bf16[128,3584]{1,0:T(8,128)(2,1)S(1)} %add_convert_fusion.3), channel_id=1, source_target_pairs={{0,8},{8,16},{16,24},{12,4},{20,12},{28,20},{1,9},{9,17},{17,25},{... | collective-permute-start | bytes 2752520 | tf_op jit(solution)/shard_map/ppermute | solution.py:184
  108.3 19.3 %collective-permute-start.22 = (bf16[128,3584]{1,0:T(8,128)(2,1)S(1)}, bf16[128,3584]{1,0:T(8,128)(2,1)S(1)}, u32[]{:S(2)}, u32[]{:S(2)}) collective-permute-start(bf16[128,3584]{1,0:T(8,128)(2,1)S(1)} %add_convert_fusion.2), channel_id=1, source_target_pairs={{0,8},{8,16},{16,24},{12,4},{20,12},{28,20},{1,9},{9,17},{17,25},{... | collective-permute-start | bytes 2752520 | tf_op jit(solution)/shard_map/ppermute | solution.py:184
  118.2 19.2 %collective-permute-start.21 = (bf16[128,3584]{1,0:T(8,128)(2,1)S(1)}, bf16[128,3584]{1,0:T(8,128)(2,1)S(1)}, u32[]{:S(2)}, u32[]{:S(2)}) collective-permute-start(bf16[128,3584]{1,0:T(8,128)(2,1)S(1)} %add_convert_fusion.1), channel_id=1, source_target_pairs={{0,8},{8,16},{16,24},{12,4},{20,12},{28,20},{1,9},{9,17},{17,25},{... | collective-permute-start | bytes 2752520 | tf_op jit(solution)/shard_map/ppermute | solution.py:184
  137.4 1.6 copy-start.16
  137.5 2.6 %collective-permute-start.23 = (bf16[128,3584]{1,0:T(8,128)(2,1)S(1)}, bf16[128,3584]{1,0:T(8,128)(2,1)}, u32[]{:S(2)}, u32[]{:S(2)}) collective-permute-start(bf16[128,3584]{1,0:T(8,128)(2,1)S(1)} %collective-permute-done.21), channel_id=1, source_target_pairs={{0,4},{4,0},{8,12},{12,8},{16,20},{20,16},{24,28},{28,24},{1,5},{5... | collective-permute-start | bytes 2752520 | tf_op jit(solution)/shard_map/ppermute | solution.py:175
  137.5 2.6 %slice-start.1 = ((bf16[512,3584]{1,0:T(8,128)(2,1)}), bf16[128,3584]{1,0:T(8,128)(2,1)S(1)}, s32[]{:S(2)}) async-start(bf16[512,3584]{1,0:T(8,128)(2,1)} %copy-done.5), calls=%async_computation.1 | async-start | bytes 1835008 | tf_op jit(solution)/shard_map/slice | solution.py:230
  142.6 2.3 collective-permute-start.24
  142.8 3.3 %copy-start.10 = (f32[64,7168]{1,0:T(8,128)S(1)}, f32[64,7168]{1,0:T(8,128)}, u32[]{:S(2)}) copy-start(f32[64,7168]{1,0:T(8,128)} %shard_map.81) | copy-start | bytes 5505028
  142.8 15.6 %collective-permute-start.29 = (bf16[128,3584]{1,0:T(8,128)(2,1)}, bf16[128,3584]{1,0:T(8,128)(2,1)S(1)}, u32[]{:S(2)}, u32[]{:S(2)}) collective-permute-start(bf16[128,3584]{1,0:T(8,128)(2,1)} %add_convert_fusion), channel_id=1, source_target_pairs={{0,8},{8,16},{16,24},{12,4},{20,12},{28,20},{1,9},{9,17},{17,25},{... | collective-permute-start | bytes 2752520 | tf_op jit(solution)/shard_map/ppermute | solution.py:184
  145.9 15.8 %slice-start = ((bf16[512,3584]{1,0:T(8,128)(2,1)}), bf16[128,3584]{1,0:T(8,128)(2,1)S(1)}, s32[]{:S(2)}) async-start(bf16[512,3584]{1,0:T(8,128)(2,1)} %copy-done.3), calls=%async_computation | async-start | bytes 1835008 | tf_op jit(solution)/shard_map/slice | solution.py:230
  146.0 15.8 %copy-start.6 = (f32[64,7168]{1,0:T(8,128)S(1)}, f32[64,7168]{1,0:T(8,128)}, u32[]{:S(2)}) copy-start(f32[64,7168]{1,0:T(8,128)} %param.8) | copy-start | bytes 5505028
  146.0 15.8 %copy-start.7 = (f32[64,7168]{1,0:T(8,128)S(1)}, f32[64,7168]{1,0:T(8,128)}, u32[]{:S(2)}) copy-start(f32[64,7168]{1,0:T(8,128)} %param.9) | copy-start | bytes 5505028
  146.1 16.6 %copy-start.12 = (bf16[128,3584]{1,0:T(8,128)(2,1)}, bf16[128,3584]{1,0:T(8,128)(2,1)S(1)}, u32[]{:S(2)}) copy-start(bf16[128,3584]{1,0:T(8,128)(2,1)S(1)} %pad_maximum_fusion) | copy-start | bytes 2752516
  158.4 3.3 %collective-permute-start.30 = (bf16[128,3584]{1,0:T(8,128)(2,1)S(1)}, bf16[128,3584]{1,0:T(8,128)(2,1)S(1)}, u32[]{:S(2)}, u32[]{:S(2)}) collective-permute-start(bf16[128,3584]{1,0:T(8,128)(2,1)S(1)} %collective-permute-done.29), channel_id=1, source_target_pairs={{0,4},{4,0},{8,12},{12,8},{16,20},{20,16},{24,28},{28,24},{1,5},{5... | collective-permute-start | bytes 2752520 | tf_op jit(solution)/shard_map/ppermute | solution.py:175
  158.4 15.4 %collective-permute-start.25 = (bf16[128,3584]{1,0:T(8,128)(2,1)S(1)}, bf16[128,3584]{1,0:T(8,128)(2,1)}, u32[]{:S(2)}, u32[]{:S(2)}) collective-permute-start(bf16[128,3584]{1,0:T(8,128)(2,1)S(1)} %pad_maximum_fusion), channel_id=1, source_target_pairs={{0,8},{8,16},{16,24},{12,4},{20,12},{28,20},{1,9},{9,17},{17,25},{... | collective-permute-start | bytes 2752520 | tf_op jit(solution)/shard_map/ppermute | solution.py:184
  162.6 13.1 %collective-permute-start.31 = (bf16[64,3584]{1,0:T(8,128)(2,1)S(1)}, bf16[64,3584]{1,0:T(8,128)(2,1)S(1)}, u32[]{:S(2)}, u32[]{:S(2)}) collective-permute-start(bf16[64,3584]{1,0:T(8,128)(2,1)S(1)} %get-tuple-element.117), channel_id=1, source_target_pairs={{0,4},{4,0},{8,12},{12,8},{16,20},{20,16},{24,28},{28,24},{1,5},{5... | collective-permute-start | bytes 1376264 | tf_op jit(solution)/shard_map/ppermute | solution.py:175
  173.8 15.6 %collective-permute-start.26 = (bf16[128,3584]{1,0:T(8,128)(2,1)}, bf16[128,3584]{1,0:T(8,128)(2,1)}, u32[]{:S(2)}, u32[]{:S(2)}) collective-permute-start(bf16[128,3584]{1,0:T(8,128)(2,1)} %collective-permute-done.25), channel_id=1, source_target_pairs={{0,8},{8,16},{16,24},{12,4},{20,12},{28,20},{1,9},{9,17},{17,25},{... | collective-permute-start | bytes 2752520 | tf_op jit(solution)/shard_map/ppermute | solution.py:184
  175.9 23.4 %copy-start.14 = (bf16[128,3584]{1,0:T(8,128)(2,1)}, bf16[128,3584]{1,0:T(8,128)(2,1)S(1)}, u32[]{:S(2)}) copy-start(bf16[128,3584]{1,0:T(8,128)(2,1)S(1)} %pad_maximum_fusion.1) | copy-start | bytes 2752516
  175.9 23.3 %collective-permute-start.34 = (bf16[128,3584]{1,0:T(8,128)(2,1)S(1)}, bf16[128,3584]{1,0:T(8,128)(2,1)}, u32[]{:S(2)}, u32[]{:S(2)}) collective-permute-start(bf16[128,3584]{1,0:T(8,128)(2,1)S(1)} %pad_maximum_fusion.1), channel_id=1, source_target_pairs={{0,8},{8,16},{16,24},{12,4},{20,12},{28,20},{1,9},{9,17},{17,25},{... | collective-permute-start | bytes 2752520 | tf_op jit(solution)/shard_map/ppermute | solution.py:184
  189.4 19.7 %collective-permute-start.27 = (bf16[128,3584]{1,0:T(8,128)(2,1)}, bf16[128,3584]{1,0:T(8,128)(2,1)}, u32[]{:S(2)}, u32[]{:S(2)}) collective-permute-start(bf16[128,3584]{1,0:T(8,128)(2,1)} %collective-permute-done.26), channel_id=1, source_target_pairs={{0,8},{8,16},{16,24},{12,4},{20,12},{28,20},{1,9},{9,17},{17,25},{... | collective-permute-start | bytes 2752520 | tf_op jit(solution)/shard_map/ppermute | solution.py:184
  191.3 27.6 %collective-permute-start.28 = (bf16[128,3584]{1,0:T(8,128)(2,1)}, bf16[128,3584]{1,0:T(8,128)(2,1)}, u32[]{:S(2)}, u32[]{:S(2)}) collective-permute-start(bf16[128,3584]{1,0:T(8,128)(2,1)} %collective-permute-done.25), channel_id=1, source_target_pairs={{0,4},{4,0},{8,12},{12,8},{16,20},{20,16},{24,28},{28,24},{1,5},{5... | collective-permute-start | bytes 2752520 | tf_op jit(solution)/shard_map/ppermute | solution.py:175
  191.5 1.2 copy-start.11
  199.2 19.7 %collective-permute-start.35 = (bf16[128,3584]{1,0:T(8,128)(2,1)}, bf16[128,3584]{1,0:T(8,128)(2,1)}, u32[]{:S(2)}, u32[]{:S(2)}) collective-permute-start(bf16[128,3584]{1,0:T(8,128)(2,1)} %collective-permute-done.34), channel_id=1, source_target_pairs={{0,8},{8,16},{16,24},{12,4},{20,12},{28,20},{1,9},{9,17},{17,25},{... | collective-permute-start | bytes 2752520 | tf_op jit(solution)/shard_map/ppermute | solution.py:184
  201.2 19.7 %collective-permute-start.32 = (bf16[128,3584]{1,0:T(8,128)(2,1)}, bf16[128,3584]{1,0:T(8,128)(2,1)}, u32[]{:S(2)}, u32[]{:S(2)}) collective-permute-start(bf16[128,3584]{1,0:T(8,128)(2,1)} %collective-permute-done.26), channel_id=1, source_target_pairs={{0,4},{4,0},{8,12},{12,8},{16,20},{20,16},{24,28},{28,24},{1,5},{5... | collective-permute-start | bytes 2752520 | tf_op jit(solution)/shard_map/ppermute | solution.py:175
  209.1 11.8 %collective-permute-start.33 = (bf16[128,3584]{1,0:T(8,128)(2,1)}, bf16[128,3584]{1,0:T(8,128)(2,1)}, u32[]{:S(2)}, u32[]{:S(2)}) collective-permute-start(bf16[128,3584]{1,0:T(8,128)(2,1)} %collective-permute-done.27), channel_id=1, source_target_pairs={{0,4},{4,0},{8,12},{12,8},{16,20},{20,16},{24,28},{28,24},{1,5},{5... | collective-permute-start | bytes 2752520 | tf_op jit(solution)/shard_map/ppermute | solution.py:175
  209.1 15.7 %copy-start.13 = (bf16[128,3584]{1,0:T(8,128)(2,1)S(1)}, bf16[128,3584]{1,0:T(8,128)(2,1)}, u32[]{:S(2)}) copy-start(bf16[128,3584]{1,0:T(8,128)(2,1)} %copy-done.12) | copy-start | bytes 2752516
  209.1 25.5 %collective-permute-start.37 = (bf16[128,3584]{1,0:T(8,128)(2,1)}, bf16[128,3584]{1,0:T(8,128)(2,1)S(1)}, u32[]{:S(2)}, u32[]{:S(2)}) collective-permute-start(bf16[128,3584]{1,0:T(8,128)(2,1)} %collective-permute-done.34), channel_id=1, source_target_pairs={{0,4},{4,0},{8,12},{12,8},{16,20},{20,16},{24,28},{28,24},{1,5},{5... | collective-permute-start | bytes 2752520 | tf_op jit(solution)/shard_map/ppermute | solution.py:175
  218.9 15.7 %collective-permute-start.38 = (bf16[128,3584]{1,0:T(8,128)(2,1)}, bf16[128,3584]{1,0:T(8,128)(2,1)S(1)}, u32[]{:S(2)}, u32[]{:S(2)}) collective-permute-start(bf16[128,3584]{1,0:T(8,128)(2,1)} %collective-permute-done.35), channel_id=1, source_target_pairs={{0,4},{4,0},{8,12},{12,8},{16,20},{20,16},{24,28},{28,24},{1,5},{5... | collective-permute-start | bytes 2752520 | tf_op jit(solution)/shard_map/ppermute | solution.py:175
  218.9 15.5 %collective-permute-start.36 = (bf16[128,3584]{1,0:T(8,128)(2,1)}, bf16[128,3584]{1,0:T(8,128)(2,1)S(1)}, u32[]{:S(2)}, u32[]{:S(2)}) collective-permute-start(bf16[128,3584]{1,0:T(8,128)(2,1)} %collective-permute-done.35), channel_id=1, source_target_pairs={{0,8},{8,16},{16,24},{12,4},{20,12},{28,20},{1,9},{9,17},{17,25},{... | collective-permute-start | bytes 2752520 | tf_op jit(solution)/shard_map/ppermute | solution.py:184
  224.7 9.7 %copy-start.8 = (f32[64,7168]{1,0:T(8,128)S(1)}, f32[64,7168]{1,0:T(8,128)}, u32[]{:S(2)}) copy-start(f32[64,7168]{1,0:T(8,128)} %shard_map.82) | copy-start | bytes 5505028
  234.4 2.5 %collective-permute-start.39 = (bf16[128,3584]{1,0:T(8,128)(2,1)S(1)}, bf16[128,3584]{1,0:T(8,128)(2,1)S(1)}, u32[]{:S(2)}, u32[]{:S(2)}) collective-permute-start(bf16[128,3584]{1,0:T(8,128)(2,1)S(1)} %collective-permute-done.36), channel_id=1, source_target_pairs={{0,4},{4,0},{8,12},{12,8},{16,20},{20,16},{24,28},{28,24},{1,5},{5... | collective-permute-start | bytes 2752520 | tf_op jit(solution)/shard_map/ppermute | solution.py:175
  234.5 5.0 %copy-start.9 = (f32[64,7168]{1,0:T(8,128)}, f32[64,7168]{1,0:T(8,128)S(1)}, u32[]{:S(2)}) copy-start(f32[64,7168]{1,0:T(8,128)S(1)} %constant_dynamic-update-slice_fusion.2) | copy-start | bytes 5505028
  234.5 5.0 %copy-start.15 = (bf16[128,3584]{1,0:T(8,128)(2,1)S(1)}, bf16[128,3584]{1,0:T(8,128)(2,1)}, u32[]{:S(2)}) copy-start(bf16[128,3584]{1,0:T(8,128)(2,1)} %copy-done.14) | copy-start | bytes 2752516

commit v2 on v1

--- a/solution.py
+++ b/solution.py
@@ -14,6 +14,7 @@
 adam_eps = 1e-08
 
 PARTS = 2
+HALVES = 2
 UNIT = 256
 F32 = jnp.float32
 BF16 = jnp.bfloat16
@@ -22,7 +23,8 @@
 
 def split_widths(columns):
     units, parts = columns // UNIT, min(PARTS, columns // UNIT)
-    return [UNIT * (units // parts + (i < units % parts)) for i in range(parts)]
+    more = units % parts if parts == 3 else 0
+    return [UNIT * (units // parts + (more if i == 1 else 0) + (parts != 3 and i < units % parts)) for i in range(parts)]
 
 
 def params(mib):
@@ -95,34 +97,35 @@
     )(where, taken, *slabs)
 
 
-def flip(where, pieces, chips):
-    tokens, rank = pieces[0].shape
-    many = len(pieces)
+def flip(where, parts, chips):
+    many, halves = len(parts[0]), len(parts)
+    tokens, width = parts[0][0].shape
+    rank = width * halves
     rows = rank // chips
 
     def body(where_ref, *refs):
-        out = refs[many]
+        out, stage = refs[-2:]
         for j in range(many):
-            turned = refs[j][...].T
             at = pl.multiple_of(where_ref[j] * tokens, 128)
-            refs[many + 1][...] = turned
+            for h in range(halves):
+                stage[h * width : (h + 1) * width, :] = refs[h * many + j][...].T
             for i in range(chips):
                 source = pl.multiple_of(where_ref[many + i] * rows, rows)
-                out[pl.ds(i * rows, rows), pl.ds(at, tokens)] = refs[many + 1][pl.ds(source, rows), :]
+                out[pl.ds(i * rows, rows), pl.ds(at, tokens)] = stage[pl.ds(source, rows), :]
 
     return pl.pallas_call(
         body,
         grid_spec=pltpu.PrefetchScalarGridSpec(
             num_scalar_prefetch=1,
             grid=(1,),
-            in_specs=[pl.BlockSpec((tokens, rank), lambda i, where: (0, 0))] * many,
+            in_specs=[pl.BlockSpec((tokens, width), lambda i, where: (0, 0))] * (many * halves),
             out_specs=pl.BlockSpec((rank, many * tokens), lambda i, where: (0, 0)),
             scratch_shapes=[pltpu.VMEM((rank, tokens), BF16)],
         ),
         out_shape=jax.ShapeDtypeStruct((rank, many * tokens), BF16),
         compiler_params=params(16),
         cost_estimate=cost(0, 4 * rank * tokens * many),
-    )(where, *pieces)
+    )(where, *[piece for part in parts for piece in part])
 
 
 def arrange(where, pieces, choose):
@@ -197,7 +200,11 @@
         state["last"] = value
         return value
 
-    slabs = [projector] + [rotate(projector, chips - r) for r in range(1, chips)]
+    width = rank // HALVES
+    slabs = []
+    for h in range(HALVES):
+        own = projector[:, h * width : (h + 1) * width]
+        slabs.append([own] + [rotate(own, chips - r) for r in range(1, chips)])
     order = (chip + slots) % chips * 2
     order = jnp.concatenate([order + core, order + 1 - core]) * tensor + t_at
     taken = ended(gather(order.astype(jnp.int32), activations, dp, projector.shape[0]))
@@ -208,16 +215,18 @@
     (choose,) = after(choose)
     basis = ended(arrange(peers.astype(jnp.int32), basis, choose))
 
-    taken, *slabs[1:] = after(taken, *slabs[1:])
-    slabs = slabs + [swap(slab) for slab in slabs]
-    parts = project(peers.astype(jnp.int32), taken, slabs, tensor)
-    ended(parts[0])
-    total = parts[0]
-    for j in range(1, tensor):
-        total = total + exchange(parts[j], j).astype(F32)
-    piece = total.astype(BF16)
-    pieces = [piece] + [exchange(piece, j) for j in range(1, tensor)]
-    flipped = flip(jnp.concatenate([peers, slot_chip]).astype(jnp.int32), pieces, chips)
+    gathered = []
+    for held in slabs:
+        taken, *held[1:] = after(taken, *held[1:])
+        held = held + [swap(slab) for slab in held]
+        parts = project(peers.astype(jnp.int32), taken, held, tensor)
+        ended(parts[0])
+        total = parts[0]
+        for j in range(1, tensor):
+            total = total + exchange(parts[j], j).astype(F32)
+        piece = total.astype(BF16)
+        gathered.append([piece] + [exchange(piece, j) for j in range(1, tensor)])
+    flipped = flip(jnp.concatenate([peers, slot_chip]).astype(jnp.int32), gathered, chips)
     ended(flipped)
 
     widths = split_widths(columns)

time: 248 us -> 248 us (level)
  waiting for transfers between devices: 141 us -> 123 us
  starting transfers between devices: 42.1 us -> 53.7 us
  matrix products: 27 us -> 30.9 us
    ppermute x9 -> x15, waiting for transfers between devices: 23.9 us -> 7.58 us  [exchange(): return lax.ppermute(value, 'tensor', [(t, t ^ j) for t in range(tensor)])]
    ppermute x9 -> x15, starting transfers between devices: 10.7 us -> 19.8 us  [exchange(): return lax.ppermute(value, 'tensor', [(t, t ^ j) for t in range(tensor)])]
    dot_general x2, matrix products: 11.9 us -> 15.8 us  [encode(): jnp.dot(weights, cut(grad, k), preferred_element_type=F32).astype(BF16)]
    ppermute x3 -> x6, starting transfers between devices: 5.51 us -> 7.87 us  [rotate(): return lax.ppermute(value, 'dp', pairs)]
    ppermute x16 -> x20, waiting for transfers between devices: 9.7 us -> 7.54 us  [swap(): return lax.ppermute(value, 'dp', [(i, i ^ 1) for i in range(dp)])]
    pallas_call x1 -> x2, Pallas kernels: 3.84 us -> 5.5 us  [project(): pl.pallas_call(body, grid_spec=pltpu.PrefetchScalarGridSpec(num_scalar_pr...]
    ppermute x3 -> x6, waiting for transfers between devices: 8.61 us -> 9.43 us  [rotate(): return lax.ppermute(value, 'dp', pairs)]
  transfers between devices with their start and end apart: 40 -> 53, of which waited for: 27 -> 25; matrix products, arithmetic and copies ran while one was open for 10% -> 12% of each run, Pallas kernels for 4% -> 6%
where the time goes in v2:
time: 248 us; the launch traced here: 246 us
  waiting for transfers between devices  123 us (50%)
  starting transfers between devices  53.7 us (22%)
  matrix products  30.9 us (12%)
  Pallas kernels  15.1 us (6%)
  other arithmetic  15 us (6%)
  local copies, waits for them, and re-layouts  7.57 us (3%)
    ppermute x12, waiting for transfers between devices, onward(): return lax.ppermute(value, 'dp', up + down)  98.3 us
    ppermute x12, starting transfers between devices, onward(): return lax.ppermute(value, 'dp', up + down)  23.3 us
    ppermute x15, starting transfers between devices, exchange(): return lax.ppermute(value, 'tensor', [(t, t ^ j) for t in range(tensor)])  19.8 us
    dot_general x2, matrix products, encode(): jnp.dot(weights, cut(grad, k), preferred_element_type=F32).astype(BF16)  15.8 us
    dot_general x2, matrix products, decode(): jnp.dot(basis, jnp.concatenate(pieces), preferred_element_type=F32)  15.1 us
    ppermute x6, waiting for transfers between devices, rotate(): return lax.ppermute(value, 'dp', pairs)  9.43 us
    ppermute x6, starting transfers between devices, rotate(): return lax.ppermute(value, 'dp', pairs)  7.87 us
    ppermute x15, waiting for transfers between devices, exchange(): return lax.ppermute(value, 'tensor', [(t, t ^ j) for t in range(tensor)])  7.58 us
  transfers between devices with their start and end apart: 53, of which 25 were waited for; matrix products, arithmetic and copies ran while one was open for 12% of the time, Pallas kernels for 6%

profile of v2, /device:TPU:16, one launch (start us, length us, event | category | flops | bytes accessed | tf_op | source)
XLA Modules:
  0.0 246.5 jit_solution(1605752734680638812)
XLA Ops:
  0.6 1.6 collective-permute-start
  2.2 1.5 collective-permute-start.1
  5.7 3.5 %collective-permute-start.4 = (bf16[256,256]{1,0:T(8,128)(2,1)S(1)}, bf16[256,256]{1,0:T(8,128)(2,1)S(1)}, u32[]{:S(2)}, u32[]{:S(2)}) collective-permute-start(bf16[256,256]{1,0:T(8,128)(2,1)S(1)} %get-tuple-element.146.refs_0_), channel_id=1, source_target_pairs={{0,16},{4,20},{8,24},{12,28},{16,0},{20,4},{24,8},{28,12},{1,17},{... | collective-permute-start | bytes 393224 | tf_op jit(solution)/shard_map/ppermute | solution.py:182
  9.9 7.4 %shard_map.77.taken_ref = bf16[8,1024,256]{2,1,0:T(8,128)(2,1)} custom-call(s32[8]{0:T(128)} %fusion.30.where_ref, bf16[1024,8192]{1,0:T(8,128)(2,1)} %taken_ref.1), custom_call_target="tpu_custom_call" | custom-call | bytes 8388608 | tf_op jit(solution)/shard_map/pallas_call | solution.py:49
  17.6 1.2 shard_map.78
  18.9 3.6 %collective-permute-done.5.refs_3_ = bf16[256,256]{1,0:T(8,128)(2,1)S(1)} collective-permute-done((bf16[256,256]{1,0:T(8,128)(2,1)S(1)}, bf16[256,256]{1,0:T(8,128)(2,1)S(1)}, u32[]{:S(2)}, u32[]{:S(2)}) %collective-permute-start.5) | collective-permute-done | bytes 131104 | tf_op jit(solution)/shard_map/ppermute | solution.py:182
  23.0 2.4 collective-permute-start.17
  25.3 1.5 collective-permute-start.18
  26.8 2.2 copy-done
  29.0 2.8 %shard_map.79 = (f32[256,256]{1,0:T(8,128)S(1)}, bf16[256,256]{1,0:T(8,128)(2,1)S(1)}, bf16[256,256]{1,0:T(8,128)(2,1)S(1)}, bf16[256,256]{1,0:T(8,128)(2,1)S(1)}) custom-call(s32[4]{0:T(128)S(1)} %iota_xor_fusion.where_ref, bf16[8,1024,256]{2,1,0:T(8,128)(2,1)S(1)} %copy-done, bf16[256,256]{1,0:T(8,128)(2,1)S(1)} %get-tuple-element.146.refs_0_, ...), custom_call_target="tpu_custom_call" | custom-call | flops 1073741824 | bytes 5242880 | tf_op jit(solution)/shard_map/pallas_call | solution.py:81
  31.8 3.3 %collective-permute-done.17.refs_2_ = bf16[256,256]{1,0:T(8,128)(2,1)S(1)} collective-permute-done((bf16[256,256]{1,0:T(8,128)(2,1)S(1)}, bf16[256,256]{1,0:T(8,128)(2,1)S(1)}, u32[]{:S(2)}, u32[]{:S(2)}) %collective-permute-start.17) | collective-permute-done | bytes 131104 | tf_op jit(solution)/shard_map/ppermute | solution.py:182
  35.1 2.5 %collective-permute-done.18.refs_3_ = bf16[256,256]{1,0:T(8,128)(2,1)S(1)} collective-permute-done((bf16[256,256]{1,0:T(8,128)(2,1)S(1)}, bf16[256,256]{1,0:T(8,128)(2,1)S(1)}, u32[]{:S(2)}, u32[]{:S(2)}) %collective-permute-start.18) | collective-permute-done | bytes 131104 | tf_op jit(solution)/shard_map/ppermute | solution.py:182
  38.2 1.5 collective-permute-start.10
  39.7 1.5 collective-permute-start.11
  41.7 2.7 %shard_map.80 = (f32[256,256]{1,0:T(8,128)S(1)}, bf16[256,256]{1,0:T(8,128)(2,1)S(1)}, bf16[256,256]{1,0:T(8,128)(2,1)S(1)}, bf16[256,256]{1,0:T(8,128)(2,1)S(1)}) custom-call(s32[4]{0:T(128)S(1)} %iota_xor_fusion.where_ref, bf16[8,1024,256]{2,1,0:T(8,128)(2,1)S(1)} %copy-done, bf16[256,256]{1,0:T(8,128)(2,1)S(1)} %get-tuple-element.145.refs_0_, ...), custom_call_target="tpu_custom_call" | custom-call | flops 1073741824 | bytes 5242880 | tf_op jit(solution)/shard_map/pallas_call | solution.py:81
  44.4 1.6 collective-permute-start.23
  46.0 1.5 collective-permute-start.24
  48.2 1.4 collective-permute-start.13
  49.6 1.5 collective-permute-start.14
  51.2 2.2 collective-permute-start.15
  54.9 1.4 collective-permute-start.26
  57.5 1.5 collective-permute-start.28
  60.5 1.8 collective-permute-done.26.refs_5_
  62.3 2.7 %collective-permute-done.27.refs_6_ = bf16[256,256]{1,0:T(8,128)(2,1)S(1)} collective-permute-done((bf16[256,256]{1,0:T(8,128)(2,1)S(1)}, bf16[256,256]{1,0:T(8,128)(2,1)S(1)}, u32[]{:S(2)}, u32[]{:S(2)}) %collective-permute-start.27) | collective-permute-done | bytes 131104 | tf_op jit(solution)/shard_map/ppermute | solution.py:190
  66.0 7.3 %fusion.4 = bf16[512,3584]{1,0:T(8,128)(2,1)S(1)} fusion(bf16[512,1024]{1,0:T(8,128)(2,1)S(1)} %shard_map.81, bf16[1024,7168]{1,0:T(8,128)(2,1)} %param.6), kind=kOutput, calls=%fused_computation.6 | convolution fusion | flops 3759931392 | bytes 12058624 | tf_op jit(solution)/shard_map/dot_general | solution.py:250
  73.4 8.5 %fusion.7 = bf16[512,3584]{1,0:T(8,128)(2,1)S(1)} fusion(bf16[512,1024]{1,0:T(8,128)(2,1)S(1)} %shard_map.81, bf16[1024,7168]{1,0:T(8,128)(2,1)} %param.6), kind=kOutput, calls=%fused_computation.7 | convolution fusion | flops 3759931392 | bytes 12058624 | tf_op jit(solution)/shard_map/dot_general | solution.py:250
  82.2 1.9 collective-permute-start.30
  84.1 4.2 %collective-permute-done.31 = bf16[512,3584]{1,0:T(8,128)(2,1)S(1)} collective-permute-done((bf16[512,3584]{1,0:T(8,128)(2,1)S(1)}, bf16[512,3584]{1,0:T(8,128)(2,1)S(1)}, u32[]{:S(2)}, u32[]{:S(2)}) %collective-permute-start.31) | collective-permute-done | bytes 3670048 | tf_op jit(solution)/shard_map/ppermute | solution.py:178
  88.7 1.9 collective-permute-start.33
  90.6 6.9 %collective-permute-done.30 = bf16[128,3584]{1,0:T(8,128)(2,1)S(1)} collective-permute-done((bf16[128,3584]{1,0:T(8,128)(2,1)S(1)}, bf16[128,3584]{1,0:T(8,128)(2,1)S(1)}, u32[]{:S(2)}, u32[]{:S(2)}) %collective-permute-start.30) | collective-permute-done | bytes 917536 | tf_op jit(solution)/shard_map/ppermute | solution.py:187
  97.8 1.9 collective-permute-start.32
  99.8 7.6 %collective-permute-done.33 = bf16[128,3584]{1,0:T(8,128)(2,1)S(1)} collective-permute-done((bf16[128,3584]{1,0:T(8,128)(2,1)S(1)}, bf16[128,3584]{1,0:T(8,128)(2,1)S(1)}, u32[]{:S(2)}, u32[]{:S(2)}) %collective-permute-start.33) | collective-permute-done | bytes 917536 | tf_op jit(solution)/shard_map/ppermute | solution.py:187
  107.7 1.9 collective-permute-start.35
  109.7 7.5 %collective-permute-done.32 = bf16[128,3584]{1,0:T(8,128)(2,1)S(1)} collective-permute-done((bf16[128,3584]{1,0:T(8,128)(2,1)S(1)}, bf16[128,3584]{1,0:T(8,128)(2,1)S(1)}, u32[]{:S(2)}, u32[]{:S(2)}) %collective-permute-start.32) | collective-permute-done | bytes 917536 | tf_op jit(solution)/shard_map/ppermute | solution.py:187
  117.5 1.9 collective-permute-start.34
  119.4 7.6 %collective-permute-done.35 = bf16[128,3584]{1,0:T(8,128)(2,1)S(1)} collective-permute-done((bf16[128,3584]{1,0:T(8,128)(2,1)S(1)}, bf16[128,3584]{1,0:T(8,128)(2,1)S(1)}, u32[]{:S(2)}, u32[]{:S(2)}) %collective-permute-start.35) | collective-permute-done | bytes 917536 | tf_op jit(solution)/shard_map/ppermute | solution.py:187
  127.0 1.3 add_convert_fusion
  128.3 8.5 %collective-permute-done.34 = bf16[128,3584]{1,0:T(8,128)(2,1)S(1)} collective-permute-done((bf16[128,3584]{1,0:T(8,128)(2,1)S(1)}, bf16[128,3584]{1,0:T(8,128)(2,1)S(1)}, u32[]{:S(2)}, u32[]{:S(2)}) %collective-permute-start.34) | collective-permute-done | bytes 917536 | tf_op jit(solution)/shard_map/ppermute | solution.py:187
  136.8 1.6 slice.89
  139.4 2.5 %divide_convert_fusion.1 = (bf16[64,3584]{1,0:T(8,128)(2,1)S(1)}, f32[64,3584]{1,0:T(8,128)S(1)}, f32[64,3584]{1,0:T(8,128)S(1)}) fusion(bf16[128,3584]{1,0:T(8,128)(2,1)} %collective-permute-done.36, s32[]{:T(128)S(6)} %select_n.109, bf16[128,3584]{1,0:T(8,128)(2,1)} %copy-done.16, bf16[128,3584]{1,0:T(8,128)(2,1)S(1)} %slice-done.1, ...), kind=kLoop, calls=%fused_computation.39 | loop fusion | flops 4358144 | bytes 5963780 | tf_op jit(solution)/shard_map/convert_element_type | solution.py:272
  142.2 2.2 collective-permute-start.42
  145.7 12.1 %collective-permute-done.42 = bf16[128,3584]{1,0:T(8,128)(2,1)S(1)} collective-permute-done((bf16[128,3584]{1,0:T(8,128)(2,1)}, bf16[128,3584]{1,0:T(8,128)(2,1)S(1)}, u32[]{:S(2)}, u32[]{:S(2)}) %collective-permute-start.42) | collective-permute-done | bytes 917536 | tf_op jit(solution)/shard_map/ppermute | solution.py:187
  157.8 1.9 collective-permute-start.38
  159.7 1.2 slice.93
  162.4 10.8 %collective-permute-done.38 = bf16[128,3584]{1,0:T(8,128)(2,1)} collective-permute-done((bf16[128,3584]{1,0:T(8,128)(2,1)S(1)}, bf16[128,3584]{1,0:T(8,128)(2,1)}, u32[]{:S(2)}, u32[]{:S(2)}) %collective-permute-start.38) | collective-permute-done | bytes 917536 | tf_op jit(solution)/shard_map/ppermute | solution.py:187
  173.2 1.9 collective-permute-start.39
  175.3 1.9 collective-permute-start.47
  177.2 11.6 %collective-permute-done.39 = bf16[128,3584]{1,0:T(8,128)(2,1)} collective-permute-done((bf16[128,3584]{1,0:T(8,128)(2,1)}, bf16[128,3584]{1,0:T(8,128)(2,1)}, u32[]{:S(2)}, u32[]{:S(2)}) %collective-permute-start.39) | collective-permute-done | bytes 917536 | tf_op jit(solution)/shard_map/ppermute | solution.py:187
  188.8 1.9 collective-permute-start.40
  190.9 1.2 copy-done.11
  192.1 6.5 %collective-permute-done.47 = bf16[128,3584]{1,0:T(8,128)(2,1)} collective-permute-done((bf16[128,3584]{1,0:T(8,128)(2,1)S(1)}, bf16[128,3584]{1,0:T(8,128)(2,1)}, u32[]{:S(2)}, u32[]{:S(2)}) %collective-permute-start.47) | collective-permute-done | bytes 917536 | tf_op jit(solution)/shard_map/ppermute | solution.py:187
  198.6 1.9 collective-permute-start.48
  200.6 7.8 %collective-permute-done.40 = bf16[128,3584]{1,0:T(8,128)(2,1)} collective-permute-done((bf16[128,3584]{1,0:T(8,128)(2,1)}, bf16[128,3584]{1,0:T(8,128)(2,1)}, u32[]{:S(2)}, u32[]{:S(2)}) %collective-permute-start.40) | collective-permute-done | bytes 917536 | tf_op jit(solution)/shard_map/ppermute | solution.py:187
  208.9 9.3 %collective-permute-done.48 = bf16[128,3584]{1,0:T(8,128)(2,1)} collective-permute-done((bf16[128,3584]{1,0:T(8,128)(2,1)}, bf16[128,3584]{1,0:T(8,128)(2,1)}, u32[]{:S(2)}, u32[]{:S(2)}) %collective-permute-start.48) | collective-permute-done | bytes 917536 | tf_op jit(solution)/shard_map/ppermute | solution.py:187
  218.3 1.9 collective-permute-start.49
  220.2 1.3 broadcast_select_fusion.5
  221.5 1.3 broadcast_select_fusion.3
  222.8 1.3 broadcast_select_fusion.1
  224.1 7.6 %convolution_dynamic-update-slice_fusion.1 = f32[1024,7168]{1,0:T(8,128)} fusion(f32[1024,7168]{1,0:T(8,128)} %shard_map.76, bf16[1024,512]{1,0:T(8,128)(2,1)S(1)} %shard_map.78, bf16[128,3584]{1,0:T(8,128)(2,1)S(1)} %broadcast_select_fusion.1, bf16[128,3584]{1,0:T(8,128)(2,1)S(1)} %broadcast_select_fusion.3, ...), kind=kOutput, calls=%fused_computation.1 | convolution fusion | flops 3772776448 | bytes 19398656 | tf_op jit(solution)/shard_map/dot_general | solution.py:293
  231.7 2.1 collective-permute-done.49
  233.9 2.3 collective-permute-done.52
  236.3 1.3 broadcast_select_fusion.2
  237.6 1.3 broadcast_select_fusion
  238.9 7.6 %convolution_dynamic-update-slice_fusion = f32[1024,7168]{1,0:T(8,128)} fusion(f32[1024,7168]{1,0:T(8,128)} %convolution_dynamic-update-slice_fusion.1, bf16[1024,512]{1,0:T(8,128)(2,1)S(1)} %shard_map.78, bf16[128,3584]{1,0:T(8,128)(2,1)S(1)} %broadcast_select_fusion, bf16[128,3584]{1,0:T(8,128)(2,1)S(1)} %broadcast_select_fusion.2, ...), kind=kOutput, calls=%fused_computation | convolution fusion | flops 3772776448 | bytes 19398656 | tf_op jit(solution)/shard_map/dot_general | solution.py:293
  (126 shorter events, 17.0 us)
Async XLA Ops:
  0.6 16.8 %collective-permute-start = (bf16[256,512]{1,0:T(8,128)(2,1)}, bf16[256,512]{1,0:T(8,128)(2,1)S(1)}, u32[]{:S(2)}, u32[]{:S(2)}) collective-permute-start(bf16[256,512]{1,0:T(8,128)(2,1)} %refs_0_.1), channel_id=1, source_target_pairs={{0,1},{1,0},{2,3},{3,2},{4,5},{5,4},{6,7},{7,6},{8,9},{9,8},{10,11... | collective-permute-start | bytes 786440 | tf_op jit(solution)/shard_map/ppermute | solution.py:190
  2.2 15.3 %collective-permute-start.1 = (bf16[256,512]{1,0:T(8,128)(2,1)}, bf16[256,512]{1,0:T(8,128)(2,1)S(1)}, u32[]{:S(2)}, u32[]{:S(2)}) collective-permute-start(bf16[256,512]{1,0:T(8,128)(2,1)} %refs_0_.1), channel_id=1, source_target_pairs={{0,2},{1,3},{2,0},{3,1},{4,6},{5,7},{6,4},{7,5},{8,10},{9,11},{10,... | collective-permute-start | bytes 786440 | tf_op jit(solution)/shard_map/ppermute | solution.py:190
  3.7 13.9 %collective-permute-start.2 = (bf16[256,512]{1,0:T(8,128)(2,1)}, bf16[256,512]{1,0:T(8,128)(2,1)S(1)}, u32[]{:S(2)}, u32[]{:S(2)}) collective-permute-start(bf16[256,512]{1,0:T(8,128)(2,1)} %refs_0_.1), channel_id=1, source_target_pairs={{0,3},{1,2},{2,1},{3,0},{4,7},{5,6},{6,5},{7,4},{8,11},{9,10},{10,... | collective-permute-start | bytes 786440 | tf_op jit(solution)/shard_map/ppermute | solution.py:190
  5.2 13.7 %collective-permute-start.3 = (bf16[256,256]{1,0:T(8,128)(2,1)S(1)}, bf16[256,256]{1,0:T(8,128)(2,1)S(1)}, u32[]{:S(2)}, u32[]{:S(2)}) collective-permute-start(bf16[256,256]{1,0:T(8,128)(2,1)S(1)} %get-tuple-element.146.refs_0_), channel_id=1, source_target_pairs={{0,24},{4,28},{8,0},{12,4},{16,8},{20,12},{24,16},{28,20},{1,25},{... | collective-permute-start | bytes 393224 | tf_op jit(solution)/shard_map/ppermute | solution.py:182
  5.7 13.2 %collective-permute-start.4 = (bf16[256,256]{1,0:T(8,128)(2,1)S(1)}, bf16[256,256]{1,0:T(8,128)(2,1)S(1)}, u32[]{:S(2)}, u32[]{:S(2)}) collective-permute-start(bf16[256,256]{1,0:T(8,128)(2,1)S(1)} %get-tuple-element.146.refs_0_), channel_id=1, source_target_pairs={{0,16},{4,20},{8,24},{12,28},{16,0},{20,4},{24,8},{28,12},{1,17},{... | collective-permute-start | bytes 393224 | tf_op jit(solution)/shard_map/ppermute | solution.py:182
  17.4 5.0 %collective-permute-start.5 = (bf16[256,256]{1,0:T(8,128)(2,1)S(1)}, bf16[256,256]{1,0:T(8,128)(2,1)S(1)}, u32[]{:S(2)}, u32[]{:S(2)}) collective-permute-start(bf16[256,256]{1,0:T(8,128)(2,1)S(1)} %get-tuple-element.146.refs_0_), channel_id=1, source_target_pairs={{0,8},{4,12},{8,16},{12,20},{16,24},{20,28},{24,0},{28,4},{1,9},{5... | collective-permute-start | bytes 393224 | tf_op jit(solution)/shard_map/ppermute | solution.py:182
  17.5 5.5 %collective-permute-start.6 = (bf16[256,256]{1,0:T(8,128)(2,1)S(1)}, bf16[256,256]{1,0:T(8,128)(2,1)S(1)}, u32[]{:S(2)}, u32[]{:S(2)}) collective-permute-start(bf16[256,256]{1,0:T(8,128)(2,1)S(1)} %get-tuple-element.146.refs_0_), channel_id=1, source_target_pairs={{0,4},{4,0},{8,12},{12,8},{16,20},{20,16},{24,28},{28,24},{1,5},{5... | collective-permute-start | bytes 393224 | tf_op jit(solution)/shard_map/ppermute | solution.py:178
  22.4 2.9 %collective-permute-start.7 = (bf16[256,256]{1,0:T(8,128)(2,1)S(1)}, bf16[256,256]{1,0:T(8,128)(2,1)S(1)}, u32[]{:S(2)}, u32[]{:S(2)}) collective-permute-start(bf16[256,256]{1,0:T(8,128)(2,1)S(1)} %collective-permute-done.3.refs_1_), channel_id=1, source_target_pairs={{0,4},{4,0},{8,12},{12,8},{16,20},{20,16},{24,28},{28,24},{1,5},{5... | collective-permute-start | bytes 393224 | tf_op jit(solution)/shard_map/ppermute | solution.py:178
  22.4 4.3 %collective-permute-start.8 = (bf16[256,256]{1,0:T(8,128)(2,1)S(1)}, bf16[256,256]{1,0:T(8,128)(2,1)S(1)}, u32[]{:S(2)}, u32[]{:S(2)}) collective-permute-start(bf16[256,256]{1,0:T(8,128)(2,1)S(1)} %collective-permute-done.4.refs_2_), channel_id=1, source_target_pairs={{0,4},{4,0},{8,12},{12,8},{16,20},{20,16},{24,28},{28,24},{1,5},{5... | collective-permute-start | bytes 393224 | tf_op jit(solution)/shard_map/ppermute | solution.py:178
  22.9 3.8 %collective-permute-start.9 = (bf16[256,256]{1,0:T(8,128)(2,1)S(1)}, bf16[256,256]{1,0:T(8,128)(2,1)S(1)}, u32[]{:S(2)}, u32[]{:S(2)}) collective-permute-start(bf16[256,256]{1,0:T(8,128)(2,1)S(1)} %collective-permute-done.5.refs_3_), channel_id=1, source_target_pairs={{0,4},{4,0},{8,12},{12,8},{16,20},{20,16},{24,28},{28,24},{1,5},{5... | collective-permute-start | bytes 393224 | tf_op jit(solution)/shard_map/ppermute | solution.py:178
  23.0 8.8 %collective-permute-start.16 = (bf16[256,256]{1,0:T(8,128)(2,1)S(1)}, bf16[256,256]{1,0:T(8,128)(2,1)S(1)}, u32[]{:S(2)}, u32[]{:S(2)}) collective-permute-start(bf16[256,256]{1,0:T(8,128)(2,1)S(1)} %get-tuple-element.145.refs_0_), channel_id=1, source_target_pairs={{0,24},{4,28},{8,0},{12,4},{16,8},{20,12},{24,16},{28,20},{1,25},{... | collective-permute-start | bytes 393224 | tf_op jit(solution)/shard_map/ppermute | solution.py:182
  23.0 12.1 %collective-permute-start.17 = (bf16[256,256]{1,0:T(8,128)(2,1)S(1)}, bf16[256,256]{1,0:T(8,128)(2,1)S(1)}, u32[]{:S(2)}, u32[]{:S(2)}) collective-permute-start(bf16[256,256]{1,0:T(8,128)(2,1)S(1)} %get-tuple-element.145.refs_0_), channel_id=1, source_target_pairs={{0,16},{4,20},{8,24},{12,28},{16,0},{20,4},{24,8},{28,12},{1,17},{... | collective-permute-start | bytes 393224 | tf_op jit(solution)/shard_map/ppermute | solution.py:182
  25.3 12.3 %collective-permute-start.18 = (bf16[256,256]{1,0:T(8,128)(2,1)S(1)}, bf16[256,256]{1,0:T(8,128)(2,1)S(1)}, u32[]{:S(2)}, u32[]{:S(2)}) collective-permute-start(bf16[256,256]{1,0:T(8,128)(2,1)S(1)} %get-tuple-element.145.refs_0_), channel_id=1, source_target_pairs={{0,8},{4,12},{8,16},{12,20},{16,24},{20,28},{24,0},{28,4},{1,9},{5... | collective-permute-start | bytes 393224 | tf_op jit(solution)/shard_map/ppermute | solution.py:182
  26.8 12.9 %collective-permute-start.19 = (bf16[256,256]{1,0:T(8,128)(2,1)S(1)}, bf16[256,256]{1,0:T(8,128)(2,1)S(1)}, u32[]{:S(2)}, u32[]{:S(2)}) collective-permute-start(bf16[256,256]{1,0:T(8,128)(2,1)S(1)} %get-tuple-element.145.refs_0_), channel_id=1, source_target_pairs={{0,4},{4,0},{8,12},{12,8},{16,20},{20,16},{24,28},{28,24},{1,5},{5... | collective-permute-start | bytes 393224 | tf_op jit(solution)/shard_map/ppermute | solution.py:178
  37.6 3.6 %collective-permute-start.20 = (bf16[256,256]{1,0:T(8,128)(2,1)S(1)}, bf16[256,256]{1,0:T(8,128)(2,1)S(1)}, u32[]{:S(2)}, u32[]{:S(2)}) collective-permute-start(bf16[256,256]{1,0:T(8,128)(2,1)S(1)} %collective-permute-done.16.refs_1_), channel_id=1, source_target_pairs={{0,4},{4,0},{8,12},{12,8},{16,20},{20,16},{24,28},{28,24},{1,5},{5... | collective-permute-start | bytes 393224 | tf_op jit(solution)/shard_map/ppermute | solution.py:178
  37.7 4.0 %collective-permute-start.21 = (bf16[256,256]{1,0:T(8,128)(2,1)S(1)}, bf16[256,256]{1,0:T(8,128)(2,1)S(1)}, u32[]{:S(2)}, u32[]{:S(2)}) collective-permute-start(bf16[256,256]{1,0:T(8,128)(2,1)S(1)} %collective-permute-done.17.refs_2_), channel_id=1, source_target_pairs={{0,4},{4,0},{8,12},{12,8},{16,20},{20,16},{24,28},{28,24},{1,5},{5... | collective-permute-start | bytes 393224 | tf_op jit(solution)/shard_map/ppermute | solution.py:178
  38.1 3.5 %collective-permute-start.22 = (bf16[256,256]{1,0:T(8,128)(2,1)S(1)}, bf16[256,256]{1,0:T(8,128)(2,1)S(1)}, u32[]{:S(2)}, u32[]{:S(2)}) collective-permute-start(bf16[256,256]{1,0:T(8,128)(2,1)S(1)} %collective-permute-done.18.refs_3_), channel_id=1, source_target_pairs={{0,4},{4,0},{8,12},{12,8},{16,20},{20,16},{24,28},{28,24},{1,5},{5... | collective-permute-start | bytes 393224 | tf_op jit(solution)/shard_map/ppermute | solution.py:178
  38.2 9.3 %collective-permute-start.10 = (bf16[256,256]{1,0:T(8,128)(2,1)S(1)}, bf16[256,256]{1,0:T(8,128)(2,1)S(1)}, u32[]{:S(2)}, u32[]{:S(2)}) collective-permute-start(bf16[256,256]{1,0:T(8,128)(2,1)S(1)} %get-tuple-element.74), channel_id=1, source_target_pairs={{0,1},{1,0},{2,3},{3,2},{4,5},{5,4},{6,7},{7,6},{8,9},{9,8},{10,11... | collective-permute-start | bytes 393224 | tf_op jit(solution)/shard_map/ppermute | solution.py:190
  39.7 8.4 %collective-permute-start.11 = (bf16[256,256]{1,0:T(8,128)(2,1)S(1)}, bf16[256,256]{1,0:T(8,128)(2,1)S(1)}, u32[]{:S(2)}, u32[]{:S(2)}) collective-permute-start(bf16[256,256]{1,0:T(8,128)(2,1)S(1)} %get-tuple-element.75), channel_id=1, source_target_pairs={{0,2},{1,3},{2,0},{3,1},{4,6},{5,7},{6,4},{7,5},{8,10},{9,11},{10,... | collective-permute-start | bytes 393224 | tf_op jit(solution)/shard_map/ppermute | solution.py:190
  41.2 6.9 %collective-permute-start.12 = (bf16[256,256]{1,0:T(8,128)(2,1)S(1)}, bf16[256,256]{1,0:T(8,128)(2,1)S(1)}, u32[]{:S(2)}, u32[]{:S(2)}) collective-permute-start(bf16[256,256]{1,0:T(8,128)(2,1)S(1)} %get-tuple-element.76), channel_id=1, source_target_pairs={{0,3},{1,2},{2,1},{3,0},{4,7},{5,6},{6,5},{7,4},{8,11},{9,10},{10,... | collective-permute-start | bytes 393224 | tf_op jit(solution)/shard_map/ppermute | solution.py:190
  44.4 6.7 %collective-permute-start.23 = (bf16[256,256]{1,0:T(8,128)(2,1)S(1)}, bf16[256,256]{1,0:T(8,128)(2,1)S(1)}, u32[]{:S(2)}, u32[]{:S(2)}) collective-permute-start(bf16[256,256]{1,0:T(8,128)(2,1)S(1)} %get-tuple-element.82), channel_id=1, source_target_pairs={{0,1},{1,0},{2,3},{3,2},{4,5},{5,4},{6,7},{7,6},{8,9},{9,8},{10,11... | collective-permute-start | bytes 393224 | tf_op jit(solution)/shard_map/ppermute | solution.py:190
  46.0 8.3 %collective-permute-start.24 = (bf16[256,256]{1,0:T(8,128)(2,1)S(1)}, bf16[256,256]{1,0:T(8,128)(2,1)S(1)}, u32[]{:S(2)}, u32[]{:S(2)}) collective-permute-start(bf16[256,256]{1,0:T(8,128)(2,1)S(1)} %get-tuple-element.83), channel_id=1, source_target_pairs={{0,2},{1,3},{2,0},{3,1},{4,6},{5,7},{6,4},{7,5},{8,10},{9,11},{10,... | collective-permute-start | bytes 393224 | tf_op jit(solution)/shard_map/ppermute | solution.py:190
  47.5 7.3 %collective-permute-start.25 = (bf16[256,256]{1,0:T(8,128)(2,1)S(1)}, bf16[256,256]{1,0:T(8,128)(2,1)S(1)}, u32[]{:S(2)}, u32[]{:S(2)}) collective-permute-start(bf16[256,256]{1,0:T(8,128)(2,1)S(1)} %get-tuple-element.84), channel_id=1, source_target_pairs={{0,3},{1,2},{2,1},{3,0},{4,7},{5,6},{6,5},{7,4},{8,11},{9,10},{10,... | collective-permute-start | bytes 393224 | tf_op jit(solution)/shard_map/ppermute | solution.py:190
  48.2 9.3 %collective-permute-start.13 = (bf16[256,256]{1,0:T(8,128)(2,1)S(1)}, bf16[256,256]{1,0:T(8,128)(2,1)S(1)}, u32[]{:S(2)}, u32[]{:S(2)}) collective-permute-start(bf16[256,256]{1,0:T(8,128)(2,1)S(1)} %add_convert_fusion.7.refs_0_), channel_id=1, source_target_pairs={{0,1},{1,0},{2,3},{3,2},{4,5},{5,4},{6,7},{7,6},{8,9},{9,8},{10,11... | collective-permute-start | bytes 393224 | tf_op jit(solution)/shard_map/ppermute | solution.py:190
  49.6 10.3 %collective-permute-start.14 = (bf16[256,256]{1,0:T(8,128)(2,1)S(1)}, bf16[256,256]{1,0:T(8,128)(2,1)S(1)}, u32[]{:S(2)}, u32[]{:S(2)}) collective-permute-start(bf16[256,256]{1,0:T(8,128)(2,1)S(1)} %add_convert_fusion.7.refs_0_), channel_id=1, source_target_pairs={{0,2},{1,3},{2,0},{3,1},{4,6},{5,7},{6,4},{7,5},{8,10},{9,11},{10,... | collective-permute-start | bytes 393224 | tf_op jit(solution)/shard_map/ppermute | solution.py:190
  51.2 9.3 %collective-permute-start.15 = (bf16[256,256]{1,0:T(8,128)(2,1)S(1)}, bf16[256,256]{1,0:T(8,128)(2,1)S(1)}, u32[]{:S(2)}, u32[]{:S(2)}) collective-permute-start(bf16[256,256]{1,0:T(8,128)(2,1)S(1)} %add_convert_fusion.7.refs_0_), channel_id=1, source_target_pairs={{0,3},{1,2},{2,1},{3,0},{4,7},{5,6},{6,5},{7,4},{8,11},{9,10},{10,... | collective-permute-start | bytes 393224 | tf_op jit(solution)/shard_map/ppermute | solution.py:190
  54.9 7.4 %collective-permute-start.26 = (bf16[256,256]{1,0:T(8,128)(2,1)S(1)}, bf16[256,256]{1,0:T(8,128)(2,1)S(1)}, u32[]{:S(2)}, u32[]{:S(2)}) collective-permute-start(bf16[256,256]{1,0:T(8,128)(2,1)S(1)} %add_convert_fusion.6.refs_4_), channel_id=1, source_target_pairs={{0,1},{1,0},{2,3},{3,2},{4,5},{5,4},{6,7},{7,6},{8,9},{9,8},{10,11... | collective-permute-start | bytes 393224 | tf_op jit(solution)/shard_map/ppermute | solution.py:190
  56.3 8.7 %collective-permute-start.27 = (bf16[256,256]{1,0:T(8,128)(2,1)S(1)}, bf16[256,256]{1,0:T(8,128)(2,1)S(1)}, u32[]{:S(2)}, u32[]{:S(2)}) collective-permute-start(bf16[256,256]{1,0:T(8,128)(2,1)S(1)} %add_convert_fusion.6.refs_4_), channel_id=1, source_target_pairs={{0,2},{1,3},{2,0},{3,1},{4,6},{5,7},{6,4},{7,5},{8,10},{9,11},{10,... | collective-permute-start | bytes 393224 | tf_op jit(solution)/shard_map/ppermute | solution.py:190
  57.5 7.5 %collective-permute-start.28 = (bf16[256,256]{1,0:T(8,128)(2,1)S(1)}, bf16[256,256]{1,0:T(8,128)(2,1)S(1)}, u32[]{:S(2)}, u32[]{:S(2)}) collective-permute-start(bf16[256,256]{1,0:T(8,128)(2,1)S(1)} %add_convert_fusion.6.refs_4_), channel_id=1, source_target_pairs={{0,3},{1,2},{2,1},{3,0},{4,7},{5,6},{6,5},{7,4},{8,11},{9,10},{10,... | collective-permute-start | bytes 393224 | tf_op jit(solution)/shard_map/ppermute | solution.py:190
  73.3 43.9 %copy-start.4 = (bf16[512,3584]{1,0:T(8,128)(2,1)}, bf16[512,3584]{1,0:T(8,128)(2,1)S(1)}, u32[]{:S(2)}) copy-start(bf16[512,3584]{1,0:T(8,128)(2,1)S(1)} %fusion.4) | copy-start | bytes 11010052
  73.3 8.7 %collective-permute-start.29 = (bf16[512,3584]{1,0:T(8,128)(2,1)S(1)}, bf16[512,3584]{1,0:T(8,128)(2,1)S(1)}, u32[]{:S(2)}, u32[]{:S(2)}) collective-permute-start(bf16[512,3584]{1,0:T(8,128)(2,1)S(1)} %fusion.4), channel_id=1, source_target_pairs={{0,4},{4,0},{8,12},{12,8},{16,20},{20,16},{24,28},{28,24},{1,5},{5... | collective-permute-start | bytes 11010056 | tf_op jit(solution)/shard_map/ppermute | solution.py:178
  81.9 45.1 %copy-start.2 = (bf16[512,3584]{1,0:T(8,128)(2,1)}, bf16[512,3584]{1,0:T(8,128)(2,1)S(1)}, u32[]{:S(2)}) copy-start(bf16[512,3584]{1,0:T(8,128)(2,1)S(1)} %fusion.7) | copy-start | bytes 11010052
  81.9 6.5 %collective-permute-start.31 = (bf16[512,3584]{1,0:T(8,128)(2,1)S(1)}, bf16[512,3584]{1,0:T(8,128)(2,1)S(1)}, u32[]{:S(2)}, u32[]{:S(2)}) collective-permute-start(bf16[512,3584]{1,0:T(8,128)(2,1)S(1)} %fusion.7), channel_id=1, source_target_pairs={{0,4},{4,0},{8,12},{12,8},{16,20},{20,16},{24,28},{28,24},{1,5},{5... | collective-permute-start | bytes 11010056 | tf_op jit(solution)/shard_map/ppermute | solution.py:178
  82.0 35.2 %copy-start.5 = (bf16[512,3584]{1,0:T(8,128)(2,1)}, bf16[512,3584]{1,0:T(8,128)(2,1)S(1)}, u32[]{:S(2)}) copy-start(bf16[512,3584]{1,0:T(8,128)(2,1)S(1)} %collective-permute-done.29) | copy-start | bytes 11010052
  82.2 15.3 %collective-permute-start.30 = (bf16[128,3584]{1,0:T(8,128)(2,1)S(1)}, bf16[128,3584]{1,0:T(8,128)(2,1)S(1)}, u32[]{:S(2)}, u32[]{:S(2)}) collective-permute-start(bf16[128,3584]{1,0:T(8,128)(2,1)S(1)} %add_convert_fusion.5), channel_id=1, source_target_pairs={{0,8},{8,16},{16,24},{12,4},{20,12},{28,20},{1,9},{9,17},{17,25},{... | collective-permute-start | bytes 2752520 | tf_op jit(solution)/shard_map/ppermute | solution.py:187
  88.4 38.6 %copy-start.3 = (bf16[512,3584]{1,0:T(8,128)(2,1)}, bf16[512,3584]{1,0:T(8,128)(2,1)S(1)}, u32[]{:S(2)}) copy-start(bf16[512,3584]{1,0:T(8,128)(2,1)S(1)} %collective-permute-done.31) | copy-start | bytes 11010052
  88.7 18.7 %collective-permute-start.33 = (bf16[128,3584]{1,0:T(8,128)(2,1)S(1)}, bf16[128,3584]{1,0:T(8,128)(2,1)S(1)}, u32[]{:S(2)}, u32[]{:S(2)}) collective-permute-start(bf16[128,3584]{1,0:T(8,128)(2,1)S(1)} %add_convert_fusion.4), channel_id=1, source_target_pairs={{0,8},{8,16},{16,24},{12,4},{20,12},{28,20},{1,9},{9,17},{17,25},{... | collective-permute-start | bytes 2752520 | tf_op jit(solution)/shard_map/ppermute | solution.py:187
  97.8 19.3 %collective-permute-start.32 = (bf16[128,3584]{1,0:T(8,128)(2,1)S(1)}, bf16[128,3584]{1,0:T(8,128)(2,1)S(1)}, u32[]{:S(2)}, u32[]{:S(2)}) collective-permute-start(bf16[128,3584]{1,0:T(8,128)(2,1)S(1)} %add_convert_fusion.3), channel_id=1, source_target_pairs={{0,8},{8,16},{16,24},{12,4},{20,12},{28,20},{1,9},{9,17},{17,25},{... | collective-permute-start | bytes 2752520 | tf_op jit(solution)/shard_map/ppermute | solution.py:187
  107.7 19.3 %collective-permute-start.35 = (bf16[128,3584]{1,0:T(8,128)(2,1)S(1)}, bf16[128,3584]{1,0:T(8,128)(2,1)S(1)}, u32[]{:S(2)}, u32[]{:S(2)}) collective-permute-start(bf16[128,3584]{1,0:T(8,128)(2,1)S(1)} %add_convert_fusion.2), channel_id=1, source_target_pairs={{0,8},{8,16},{16,24},{12,4},{20,12},{28,20},{1,9},{9,17},{17,25},{... | collective-permute-start | bytes 2752520 | tf_op jit(solution)/shard_map/ppermute | solution.py:187
  117.5 19.3 %collective-permute-start.34 = (bf16[128,3584]{1,0:T(8,128)(2,1)S(1)}, bf16[128,3584]{1,0:T(8,128)(2,1)S(1)}, u32[]{:S(2)}, u32[]{:S(2)}) collective-permute-start(bf16[128,3584]{1,0:T(8,128)(2,1)S(1)} %add_convert_fusion.1), channel_id=1, source_target_pairs={{0,8},{8,16},{16,24},{12,4},{20,12},{28,20},{1,9},{9,17},{17,25},{... | collective-permute-start | bytes 2752520 | tf_op jit(solution)/shard_map/ppermute | solution.py:187
  136.8 2.6 %collective-permute-start.36 = (bf16[128,3584]{1,0:T(8,128)(2,1)S(1)}, bf16[128,3584]{1,0:T(8,128)(2,1)}, u32[]{:S(2)}, u32[]{:S(2)}) collective-permute-start(bf16[128,3584]{1,0:T(8,128)(2,1)S(1)} %collective-permute-done.34), channel_id=1, source_target_pairs={{0,4},{4,0},{8,12},{12,8},{16,20},{20,16},{24,28},{28,24},{1,5},{5... | collective-permute-start | bytes 2752520 | tf_op jit(solution)/shard_map/ppermute | solution.py:178
  142.0 2.4 collective-permute-start.37
  142.2 15.6 %collective-permute-start.42 = (bf16[128,3584]{1,0:T(8,128)(2,1)}, bf16[128,3584]{1,0:T(8,128)(2,1)S(1)}, u32[]{:S(2)}, u32[]{:S(2)}) collective-permute-start(bf16[128,3584]{1,0:T(8,128)(2,1)} %add_convert_fusion), channel_id=1, source_target_pairs={{0,8},{8,16},{16,24},{12,4},{20,12},{28,20},{1,9},{9,17},{17,25},{... | collective-permute-start | bytes 2752520 | tf_op jit(solution)/shard_map/ppermute | solution.py:187
  145.5 15.5 %slice-start = ((bf16[512,3584]{1,0:T(8,128)(2,1)}), bf16[128,3584]{1,0:T(8,128)(2,1)S(1)}, s32[]{:S(2)}) async-start(bf16[512,3584]{1,0:T(8,128)(2,1)} %copy-done.3), calls=%async_computation | async-start | bytes 1835008 | tf_op jit(solution)/shard_map/slice | solution.py:239
  145.5 15.5 %copy-start.6 = (f32[64,7168]{1,0:T(8,128)S(1)}, f32[64,7168]{1,0:T(8,128)}, u32[]{:S(2)}) copy-start(f32[64,7168]{1,0:T(8,128)} %param.8) | copy-start | bytes 5505028
  145.5 15.5 %copy-start.7 = (f32[64,7168]{1,0:T(8,128)S(1)}, f32[64,7168]{1,0:T(8,128)}, u32[]{:S(2)}) copy-start(f32[64,7168]{1,0:T(8,128)} %param.9) | copy-start | bytes 5505028
  145.6 16.2 %copy-start.12 = (bf16[128,3584]{1,0:T(8,128)(2,1)}, bf16[128,3584]{1,0:T(8,128)(2,1)S(1)}, u32[]{:S(2)}) copy-start(bf16[128,3584]{1,0:T(8,128)(2,1)S(1)} %pad_maximum_fusion) | copy-start | bytes 2752516
  157.8 3.2 %collective-permute-start.43 = (bf16[128,3584]{1,0:T(8,128)(2,1)S(1)}, bf16[128,3584]{1,0:T(8,128)(2,1)S(1)}, u32[]{:S(2)}, u32[]{:S(2)}) collective-permute-start(bf16[128,3584]{1,0:T(8,128)(2,1)S(1)} %collective-permute-done.42), channel_id=1, source_target_pairs={{0,4},{4,0},{8,12},{12,8},{16,20},{20,16},{24,28},{28,24},{1,5},{5... | collective-permute-start | bytes 2752520 | tf_op jit(solution)/shard_map/ppermute | solution.py:178
  157.8 15.4 %collective-permute-start.38 = (bf16[128,3584]{1,0:T(8,128)(2,1)S(1)}, bf16[128,3584]{1,0:T(8,128)(2,1)}, u32[]{:S(2)}, u32[]{:S(2)}) collective-permute-start(bf16[128,3584]{1,0:T(8,128)(2,1)S(1)} %pad_maximum_fusion), channel_id=1, source_target_pairs={{0,8},{8,16},{16,24},{12,4},{20,12},{28,20},{1,9},{9,17},{17,25},{... | collective-permute-start | bytes 2752520 | tf_op jit(solution)/shard_map/ppermute | solution.py:187
  161.8 13.3 %collective-permute-start.44 = (bf16[64,3584]{1,0:T(8,128)(2,1)S(1)}, bf16[64,3584]{1,0:T(8,128)(2,1)S(1)}, u32[]{:S(2)}, u32[]{:S(2)}) collective-permute-start(bf16[64,3584]{1,0:T(8,128)(2,1)S(1)} %get-tuple-element.133), channel_id=1, source_target_pairs={{0,4},{4,0},{8,12},{12,8},{16,20},{20,16},{24,28},{28,24},{1,5},{5... | collective-permute-start | bytes 1376264 | tf_op jit(solution)/shard_map/ppermute | solution.py:178
  173.2 15.6 %collective-permute-start.39 = (bf16[128,3584]{1,0:T(8,128)(2,1)}, bf16[128,3584]{1,0:T(8,128)(2,1)}, u32[]{:S(2)}, u32[]{:S(2)}) collective-permute-start(bf16[128,3584]{1,0:T(8,128)(2,1)} %collective-permute-done.38), channel_id=1, source_target_pairs={{0,8},{8,16},{16,24},{12,4},{20,12},{28,20},{1,9},{9,17},{17,25},{... | collective-permute-start | bytes 2752520 | tf_op jit(solution)/shard_map/ppermute | solution.py:187
  175.3 23.4 %copy-start.14 = (bf16[128,3584]{1,0:T(8,128)(2,1)}, bf16[128,3584]{1,0:T(8,128)(2,1)S(1)}, u32[]{:S(2)}) copy-start(bf16[128,3584]{1,0:T(8,128)(2,1)S(1)} %pad_maximum_fusion.1) | copy-start | bytes 2752516
  175.3 23.3 %collective-permute-start.47 = (bf16[128,3584]{1,0:T(8,128)(2,1)S(1)}, bf16[128,3584]{1,0:T(8,128)(2,1)}, u32[]{:S(2)}, u32[]{:S(2)}) collective-permute-start(bf16[128,3584]{1,0:T(8,128)(2,1)S(1)} %pad_maximum_fusion.1), channel_id=1, source_target_pairs={{0,8},{8,16},{16,24},{12,4},{20,12},{28,20},{1,9},{9,17},{17,25},{... | collective-permute-start | bytes 2752520 | tf_op jit(solution)/shard_map/ppermute | solution.py:187
  188.8 19.7 %collective-permute-start.40 = (bf16[128,3584]{1,0:T(8,128)(2,1)}, bf16[128,3584]{1,0:T(8,128)(2,1)}, u32[]{:S(2)}, u32[]{:S(2)}) collective-permute-start(bf16[128,3584]{1,0:T(8,128)(2,1)} %collective-permute-done.39), channel_id=1, source_target_pairs={{0,8},{8,16},{16,24},{12,4},{20,12},{28,20},{1,9},{9,17},{17,25},{... | collective-permute-start | bytes 2752520 | tf_op jit(solution)/shard_map/ppermute | solution.py:187
  190.7 27.6 %collective-permute-start.41 = (bf16[128,3584]{1,0:T(8,128)(2,1)}, bf16[128,3584]{1,0:T(8,128)(2,1)}, u32[]{:S(2)}, u32[]{:S(2)}) collective-permute-start(bf16[128,3584]{1,0:T(8,128)(2,1)} %collective-permute-done.38), channel_id=1, source_target_pairs={{0,4},{4,0},{8,12},{12,8},{16,20},{20,16},{24,28},{28,24},{1,5},{5... | collective-permute-start | bytes 2752520 | tf_op jit(solution)/shard_map/ppermute | solution.py:178
  198.6 19.7 %collective-permute-start.48 = (bf16[128,3584]{1,0:T(8,128)(2,1)}, bf16[128,3584]{1,0:T(8,128)(2,1)}, u32[]{:S(2)}, u32[]{:S(2)}) collective-permute-start(bf16[128,3584]{1,0:T(8,128)(2,1)} %collective-permute-done.47), channel_id=1, source_target_pairs={{0,8},{8,16},{16,24},{12,4},{20,12},{28,20},{1,9},{9,17},{17,25},{... | collective-permute-start | bytes 2752520 | tf_op jit(solution)/shard_map/ppermute | solution.py:187
  200.5 19.7 %collective-permute-start.45 = (bf16[128,3584]{1,0:T(8,128)(2,1)}, bf16[128,3584]{1,0:T(8,128)(2,1)}, u32[]{:S(2)}, u32[]{:S(2)}) collective-permute-start(bf16[128,3584]{1,0:T(8,128)(2,1)} %collective-permute-done.39), channel_id=1, source_target_pairs={{0,4},{4,0},{8,12},{12,8},{16,20},{20,16},{24,28},{28,24},{1,5},{5... | collective-permute-start | bytes 2752520 | tf_op jit(solution)/shard_map/ppermute | solution.py:178
  208.4 11.8 %collective-permute-start.46 = (bf16[128,3584]{1,0:T(8,128)(2,1)}, bf16[128,3584]{1,0:T(8,128)(2,1)}, u32[]{:S(2)}, u32[]{:S(2)}) collective-permute-start(bf16[128,3584]{1,0:T(8,128)(2,1)} %collective-permute-done.40), channel_id=1, source_target_pairs={{0,4},{4,0},{8,12},{12,8},{16,20},{20,16},{24,28},{28,24},{1,5},{5... | collective-permute-start | bytes 2752520 | tf_op jit(solution)/shard_map/ppermute | solution.py:178
  208.4 15.7 %copy-start.13 = (bf16[128,3584]{1,0:T(8,128)(2,1)S(1)}, bf16[128,3584]{1,0:T(8,128)(2,1)}, u32[]{:S(2)}) copy-start(bf16[128,3584]{1,0:T(8,128)(2,1)} %copy-done.12) | copy-start | bytes 2752516
  208.4 25.5 %collective-permute-start.50 = (bf16[128,3584]{1,0:T(8,128)(2,1)}, bf16[128,3584]{1,0:T(8,128)(2,1)S(1)}, u32[]{:S(2)}, u32[]{:S(2)}) collective-permute-start(bf16[128,3584]{1,0:T(8,128)(2,1)} %collective-permute-done.47), channel_id=1, source_target_pairs={{0,4},{4,0},{8,12},{12,8},{16,20},{20,16},{24,28},{28,24},{1,5},{5... | collective-permute-start | bytes 2752520 | tf_op jit(solution)/shard_map/ppermute | solution.py:178
  218.3 15.7 %collective-permute-start.51 = (bf16[128,3584]{1,0:T(8,128)(2,1)}, bf16[128,3584]{1,0:T(8,128)(2,1)S(1)}, u32[]{:S(2)}, u32[]{:S(2)}) collective-permute-start(bf16[128,3584]{1,0:T(8,128)(2,1)} %collective-permute-done.48), channel_id=1, source_target_pairs={{0,4},{4,0},{8,12},{12,8},{16,20},{20,16},{24,28},{28,24},{1,5},{5... | collective-permute-start | bytes 2752520 | tf_op jit(solution)/shard_map/ppermute | solution.py:178
  218.3 15.5 %collective-permute-start.49 = (bf16[128,3584]{1,0:T(8,128)(2,1)}, bf16[128,3584]{1,0:T(8,128)(2,1)S(1)}, u32[]{:S(2)}, u32[]{:S(2)}) collective-permute-start(bf16[128,3584]{1,0:T(8,128)(2,1)} %collective-permute-done.48), channel_id=1, source_target_pairs={{0,8},{8,16},{16,24},{12,4},{20,12},{28,20},{1,9},{9,17},{17,25},{... | collective-permute-start | bytes 2752520 | tf_op jit(solution)/shard_map/ppermute | solution.py:187
  224.1 9.7 %copy-start.8 = (f32[64,7168]{1,0:T(8,128)S(1)}, f32[64,7168]{1,0:T(8,128)}, u32[]{:S(2)}) copy-start(f32[64,7168]{1,0:T(8,128)} %shard_map.83) | copy-start | bytes 5505028
  233.8 2.5 %collective-permute-start.52 = (bf16[128,3584]{1,0:T(8,128)(2,1)S(1)}, bf16[128,3584]{1,0:T(8,128)(2,1)S(1)}, u32[]{:S(2)}, u32[]{:S(2)}) collective-permute-start(bf16[128,3584]{1,0:T(8,128)(2,1)S(1)} %collective-permute-done.49), channel_id=1, source_target_pairs={{0,4},{4,0},{8,12},{12,8},{16,20},{20,16},{24,28},{28,24},{1,5},{5... | collective-permute-start | bytes 2752520 | tf_op jit(solution)/shard_map/ppermute | solution.py:178
  (8 other events, 28.8 us)
